TPU v7x, 256 devices: a whole 4x4x8 slice. The times are simulated.
256 devices in a mesh: tm: 16 (over x, y_hi, core), space: 16 (over y_lo, z).
Axes of the slice: x: 4, y: 4 (y_hi: 2, y_lo: 2; y = y_hi * 2 + y_lo), z: 8, core: 2. Of those that a mesh axis runs over, the one named last changes fastest.
Arguments:
- state: float32 [32, 128, 64, 256], P('tm', 'space'), may hold values from -1.5 to 1.5
- initial: float32 [128, 64, 256], P('space'), may hold values from -1.5 to 1.5
Outputs:
- updated: float32 [32, 128, 64, 256], P('tm', 'space')
- residual: float32 [32, 128, 64, 256], P('tm', 'space')
All inputs are finite; a program needn't handle non-finite values.
Results may differ from a plain program's by a relative error of at most 0.0003.
Values sent between devices are 32-bit elements; how exact they have to be, the bound alone decides.
A program may use at most 64 MiB of HBM per device.

v0:
```python
import math

import jax
import jax.numpy as jnp
from jax import lax
from jax.sharding import PartitionSpec as P

SWEEPS = 6


alpha_value = 0.1
time_step = 0.1
couple_first = 0.4
couple_cross = 0.05
reaction_shift = 0.1
relaxation = 0.9


def shifted(block, axis, distance):
    devices = range(lax.axis_size(axis))
    route = [(i - distance, i) for i in devices if i - distance in devices]
    return lax.ppermute(block, axis, route)


def extended(block, sides, width):
    for axis, dim in sides:
        count = lax.axis_size(axis)
        forward = [(i, i + 1) for i in range(count - 1)]
        forward.append((count - 1, 0))
        backward = [(target, source) for source, target in forward]
        low = lax.ppermute(
            lax.slice_in_dim(block, block.shape[dim] - width, None, axis=dim), axis, forward
        )
        high = lax.ppermute(lax.slice_in_dim(block, 0, width, axis=dim), axis, backward)
        block = jnp.concatenate([low, block, high], axis=dim)
    return block


def cross_sum(field):
    return (
        jnp.roll(field, 1, -2)
        + jnp.roll(field, -1, -2)
        + jnp.roll(field, 1, -1)
        + jnp.roll(field, -1, -1)
    )


def phases(lefts, rights, horizon):
    products = lefts[:, None] * rights[None, :] % horizon
    return 2.0 * math.pi / horizon * products.astype(jnp.float32)


def scales(horizon):
    counter = jnp.arange(horizon)
    return jnp.power(alpha_value, counter.astype(jnp.float32) / horizon)


def mode_diagonal(modes, horizon):
    root_alpha = alpha_value ** (1.0 / horizon)
    angles = 2.0 * math.pi / horizon * modes.astype(jnp.float32)
    diag_real = (
        1.0
        - root_alpha * jnp.cos(angles)
        + reaction_shift
        + 2.0 * couple_first
        + 4.0 * couple_cross
    )
    diag_imag = root_alpha * jnp.sin(angles)
    return (diag_real, diag_imag)


def complex_entries(modes, horizon):
    diag_real, diag_imag = mode_diagonal(modes, horizon)
    magnitude = diag_real * diag_real + diag_imag * diag_imag
    inv_real = diag_real / magnitude
    inv_imag = -diag_imag / magnitude
    return (inv_real, -inv_imag, inv_imag, inv_real)


def apply_pairs(source, entries):
    upper_left, upper_right, lower_left, lower_right = [e[:, None, None, None] for e in entries]
    upper_row = upper_left * source[:, 0] + upper_right * source[:, 1]
    lower_row = lower_left * source[:, 0] + lower_right * source[:, 1]
    return jnp.stack([upper_row, lower_row], axis=1)


def body(state, initial):
    steps_local, slab_width, second, third = state.shape
    horizon = steps_local * lax.axis_size("tm")
    position = lax.axis_index("tm")
    highest = lax.Precision.HIGHEST
    carried = shifted(state[steps_local - 1], "tm", 1)
    carried = jnp.where(position == 0, initial, carried)
    before = jnp.concatenate([carried[None], state[:-1]], axis=0)
    padded = extended(state, (("space", 1),), 1)
    laplace = couple_first * (padded[:, 2:] + padded[:, :-2] - 2.0 * state) + couple_cross * (
        cross_sum(state) - 4.0 * state
    )
    residual = before - state + laplace + time_step * (state - state * state * state)
    flattened = residual.reshape(steps_local, slab_width * second, third)
    counter = jnp.arange(horizon)
    weight = scales(horizon)
    modes = jnp.where(counter == 1, horizon // 2, counter // 2)
    odd_rows = (counter % 2 == 1) & (counter != 1)
    angles = phases(modes, counter, horizon)
    basis = jnp.where(odd_rows[:, None], -jnp.sin(angles), jnp.cos(angles))
    factor = jnp.where(counter < 2, 1.0, 2.0)
    fore_rows = basis * weight[None, :]
    back_rows = (basis * factor[:, None]).T / (horizon * weight[:, None])

    def forward(pieces):
        return jnp.einsum("pn,nci->pci", fore_rows, pieces, precision=highest)

    spectra = forward(lax.all_to_all(flattened, "tm", split_axis=1, concat_axis=0, tiled=True))
    owned = lax.all_to_all(spectra, "tm", split_axis=0, concat_axis=1, tiled=True)
    pair_count = steps_local // 2
    fields = owned.reshape(pair_count, 2, slab_width, second, third)
    pair_modes = position * pair_count + jnp.arange(pair_count)
    upper_left, upper_right, lower_left, lower_right = complex_entries(pair_modes, horizon)
    lowest, unused_low = mode_diagonal(jnp.zeros_like(pair_modes), horizon)
    highest_mode, unused_high = mode_diagonal(jnp.zeros_like(pair_modes) + horizon // 2, horizon)
    leading = pair_modes == 0
    entries = (
        jnp.where(leading, 1.0 / lowest, upper_left),
        jnp.where(leading, 0.0, upper_right),
        jnp.where(leading, 0.0, lower_left),
        jnp.where(leading, 1.0 / highest_mode, lower_right),
    )
    reach = SWEEPS - 1
    widened = extended(fields, (("space", 2),), reach)
    solved = relaxation * apply_pairs(widened, entries)
    for sweep_index in range(reach):
        interior = solved[:, :, 1:-1]
        nearby = couple_first * (solved[:, :, 2:] + solved[:, :, :-2]) + couple_cross * cross_sum(
            interior
        )
        offset = sweep_index + 1
        source = widened[:, :, offset : offset + interior.shape[2]]
        solved = (1.0 - relaxation) * interior + relaxation * apply_pairs(source + nearby, entries)
    solved_rows = solved.reshape(steps_local, slab_width * second, third)

    def backward(pieces):
        return jnp.einsum("np,pci->nci", back_rows, pieces, precision=highest)

    restored = backward(lax.all_to_all(solved_rows, "tm", split_axis=1, concat_axis=0, tiled=True))
    delta = lax.all_to_all(restored, "tm", split_axis=0, concat_axis=1, tiled=True).reshape(
        state.shape
    )
    return (state + delta, residual)


def solution(mesh):
    in_specs = (P("tm", "space", None, None), P("space", None, None))
    out_specs = (P("tm", "space", None, None), P("tm", "space", None, None))
    return jax.shard_map(body, mesh=mesh, in_specs=in_specs, out_specs=out_specs, check_vma=False)
```

profile of v0, /device:TPU:1, one launch (start us, length us, event | category | flops | bytes accessed | tf_op | source)
XLA Modules:
  0.0 159.2 jit_solution(1270484051841536747)
XLA Ops:
  0.6 2.2 %slice_bitcast_fusion = (f32[8,64,256]{2,1,0:T(8,128)S(1)}, f32[1,8,64,256]{3,2,1,0:T(8,128)}) fusion(f32[2,8,64,256]{3,2,1,0:T(8,128)} %param.2), kind=kLoop, calls=%fused_computation.87 | loop fusion | bytes 2097152 | tf_op jit(solution)/shard_map/squeeze | solution.py:92
  2.8 6.2 %collective-permute-start = (f32[8,64,256]{2,1,0:T(8,128)S(1)}, f32[8,64,256]{2,1,0:T(8,128)S(1)}, u32[]{:S(2)}, u32[]{:S(2)}) collective-permute-start(f32[8,64,256]{2,1,0:T(8,128)S(1)} %get-tuple-element.64), channel_id=1, source_target_pairs={{0,16},{16,32},{32,48},{48,64},{64,80},{80,96},{96,112},{112,128},... | collective-permute-start | bytes 1572872 | tf_op jit(solution)/shard_map/ppermute | solution.py:22
  9.0 0.7 fusion.127
  9.7 5.7 %collective-permute-start.1 = (f32[2,1,64,256]{3,2,1,0:T(8,128)}, f32[2,1,64,256]{3,2,1,0:T(8,128)S(1)}, u32[]{:S(2)}, u32[]{:S(2)}) collective-permute-start(f32[2,1,64,256]{3,2,1,0:T(8,128)} %get-tuple-element.66), channel_id=1, source_target_pairs={{1,0},{2,1},{3,2},{4,3},{5,4},{6,5},{7,6},{8,7},{9,8},{10,9},{11,1... | collective-permute-start | bytes 393224 | tf_op jit(solution)/shard_map/ppermute | solution.py:34
  15.4 1.3 fusion.123
  16.7 1.2 fusion.124
  17.9 0.2 fusion.125
  18.2 0.8 copy-done.6
  19.0 2.4 %collective-permute-done.2 = f32[2,1,64,256]{3,2,1,0:T(8,128)S(1)} collective-permute-done((f32[2,1,64,256]{3,2,1,0:T(8,128)S(1)}, f32[2,1,64,256]{3,2,1,0:T(8,128)S(1)}, u32[]{:S(2)}, u32[]{:S(2)}) %collective-permute-start.2) | collective-permute-done | bytes 131104 | tf_op jit(solution)/shard_map/ppermute | solution.py:31
  21.5 1.0 fusion.29
  22.5 1.8 %copy.18 = f32[2,8,64,256]{3,0,2,1:T(2,128)} copy(f32[2,8,64,256]{3,2,1,0:T(8,128)S(1)} %fusion.29) | data formatting | bytes 2097152 | tf_op jit(solution)/shard_map/add | solution.py:99
  24.3 6.9 %all-to-all-start = ((f32[2,512,256]{2,0,1:T(2,128)}), f32[2,512,256]{2,0,1:T(2,128)S(1)}, u32[]{:S(2)}, u32[]{:S(2)}) async-start(f32[2,512,256]{2,0,1:T(2,128)} %bitcast.47), calls=%async_computation | async-start | bytes 2097152 | tf_op jit(solution)/shard_map/all_to_all | solution.py:114
  31.2 17.2 %all-to-all-done = f32[2,512,256]{2,0,1:T(2,128)S(1)} async-done(((f32[2,512,256]{2,0,1:T(2,128)}), f32[2,512,256]{2,0,1:T(2,128)S(1)}, u32[]{:S(2)}, u32[]{:S(2)}) %all-to-all-start) | async-done | bytes 1048608 | tf_op jit(solution)/shard_map/all_to_all | solution.py:114
  48.5 0.8 copy.20
  49.3 0.7 all_to_all.51
  50.0 1.1 fusion.52
  51.2 0.6 copy.21
  51.8 20.6 %all_to_all.66 = f32[32,32,256]{2,1,0:T(8,128)S(1)} all-to-all(f32[32,32,256]{2,1,0:T(8,128)S(1)} %copy.21), channel_id=1, replica_groups=mesh['tm'=16,'space'=16] {'tm'}, dimensions={0} | all-to-all | bytes 2097152 | tf_op jit(solution)/shard_map/all_to_all | solution.py:115
  72.4 0.1 copy.22
  72.5 1.0 fusion.122
  73.5 3.6 %collective-permute-start.4 = (f32[1,2,5,64,256]{4,3,2,1,0:T(8,128)S(1)}, f32[1,2,5,64,256]{4,3,2,1,0:T(8,128)}, u32[]{:S(2)}, u32[]{:S(2)}) collective-permute-start(f32[1,2,5,64,256]{4,3,2,1,0:T(8,128)S(1)} %get-tuple-element.55), channel_id=1, source_target_pairs={{1,0},{2,1},{3,2},{4,3},{5,4},{6,5},{7,6},{8,7},{9,8},{10,9},{11,1... | collective-permute-start | bytes 1966088 | tf_op jit(solution)/shard_map/ppermute | solution.py:34
  77.3 13.4 %collective-permute-done.3 = f32[1,2,5,64,256]{4,3,2,1,0:T(8,128)S(1)} collective-permute-done((f32[1,2,5,64,256]{4,3,2,1,0:T(8,128)}, f32[1,2,5,64,256]{4,3,2,1,0:T(8,128)S(1)}, u32[]{:S(2)}, u32[]{:S(2)}) %collective-permute-start.3) | collective-permute-done | bytes 655392 | tf_op jit(solution)/shard_map/ppermute | solution.py:31
  90.7 1.2 pad_maximum_fusion
  91.9 0.3 multiply_add_fusion.1
  92.3 0.3 maximum_multiply_fusion
  92.6 0.8 fusion.102
  93.4 0.5 fusion.104
  93.9 0.4 fusion.103
  94.4 2.2 %fusion.2 = f32[1,2,16,64,256]{4,3,2,1,0:T(8,128)S(1)} fusion(f32[1,2,18,64,256]{4,3,2,1,0:T(8,128)S(1)} %maximum_multiply_fusion, f32[1,2,18,64,256]{4,3,2,1,0:T(8,128)S(1)} %pad_maximum_fusion, f32[1,2,16,63,256]{4,3,2,1,0:T(8,128)S(1)} %get-tuple-element.7, f32[1,2,16,1,256]{4,3,2,1,0:T(1,128)S(1)} %get-tuple-element.9, ...), kind=kLoop, calls=%fused_computation.5 | loop fusion | flops 6291456 | bytes 16777216 | tf_op jit(solution)/shard_map/add | solution.py:139
  96.6 0.3 multiply_add_fusion.3
  96.9 0.4 fusion.3
  97.3 0.6 fusion.106
  98.0 0.5 fusion.108
  98.5 0.3 fusion.107
  98.9 1.6 %fusion.9 = f32[1,2,14,64,256]{4,3,2,1,0:T(8,128)S(1)} fusion(f32[1,2,16,64,256]{4,3,2,1,0:T(8,128)S(1)} %fusion.3, f32[1,2,18,64,256]{4,3,2,1,0:T(8,128)S(1)} %pad_maximum_fusion, f32[1,2,14,63,256]{4,3,2,1,0:T(8,128)S(1)} %get-tuple-element.17, f32[1,2,14,1,256]{4,3,2,1,0:T(1,128)S(1)} %get-tuple-element.19, ...), kind=kLoop, calls=%fused_computation.16 | loop fusion | flops 5505024 | bytes 14680064 | tf_op jit(solution)/shard_map/add | solution.py:139
  100.5 0.3 multiply_add_fusion.5
  100.8 0.3 fusion.10
  101.1 0.5 fusion.110
  101.7 0.4 fusion.112
  102.1 0.3 fusion.111
  102.4 1.2 fusion.16
  103.6 0.3 multiply_add_fusion.7
  103.9 0.3 fusion.17
  104.2 0.4 fusion.114
  104.7 0.3 fusion.116
  105.0 0.2 fusion.115
  105.2 1.1 fusion.23
  106.4 0.2 multiply_add_fusion.9
  106.5 0.2 fusion.24
  106.8 0.4 fusion.118
  107.1 0.2 fusion.120
  107.4 0.2 fusion.119
  107.6 0.8 fusion.32
  108.4 0.1 multiply_add_fusion.11
  108.5 0.2 fusion.33
  108.7 1.8 %copy.23 = f32[2,512,256]{2,0,1:T(2,128)} copy(f32[2,512,256]{2,1,0:T(8,128)S(1)} %bitcast.45) | data formatting | bytes 2097152 | tf_op jit(solution)/shard_map/reshape | solution.py:140
  110.5 6.3 %all-to-all-start.2 = ((f32[2,512,256]{2,0,1:T(2,128)}), f32[2,512,256]{2,0,1:T(2,128)S(1)}, u32[]{:S(2)}, u32[]{:S(2)}) async-start(f32[2,512,256]{2,0,1:T(2,128)} %copy.23), calls=%async_computation.2 | async-start | bytes 2097152 | tf_op jit(solution)/shard_map/all_to_all | solution.py:145
  116.8 17.2 %all-to-all-done.2 = f32[2,512,256]{2,0,1:T(2,128)S(1)} async-done(((f32[2,512,256]{2,0,1:T(2,128)}), f32[2,512,256]{2,0,1:T(2,128)S(1)}, u32[]{:S(2)}, u32[]{:S(2)}) %all-to-all-start.2) | async-done | bytes 1048608 | tf_op jit(solution)/shard_map/all_to_all | solution.py:145
  134.1 0.8 copy.25
  134.9 0.7 all_to_all.58
  135.6 1.1 fusion.54
  136.7 0.6 copy.26
  137.3 20.6 %all_to_all.67 = f32[32,32,256]{2,1,0:T(8,128)S(1)} all-to-all(f32[32,32,256]{2,1,0:T(8,128)S(1)} %copy.26), channel_id=1, replica_groups=mesh['tm'=16,'space'=16] {'tm'}, dimensions={0} | all-to-all | bytes 2097152 | tf_op jit(solution)/shard_map/all_to_all | solution.py:146
  158.0 1.1 bitcast_add_fusion
  (32 shorter events, 0.6 us)
Async XLA Ops:
  0.6 8.4 %copy-start = (f32[2,8,64,256]{3,2,1,0:T(8,128)S(1)}, f32[2,8,64,256]{3,2,1,0:T(8,128)}, u32[]{:S(2)}) copy-start(f32[2,8,64,256]{3,2,1,0:T(8,128)} %param.2) | copy-start | bytes 3145732
  2.8 15.4 %collective-permute-start = (f32[8,64,256]{2,1,0:T(8,128)S(1)}, f32[8,64,256]{2,1,0:T(8,128)S(1)}, u32[]{:S(2)}, u32[]{:S(2)}) collective-permute-start(f32[8,64,256]{2,1,0:T(8,128)S(1)} %get-tuple-element.64), channel_id=1, source_target_pairs={{0,16},{16,32},{32,48},{48,64},{64,80},{80,96},{96,112},{112,128},... | collective-permute-start | bytes 1572872 | tf_op jit(solution)/shard_map/ppermute | solution.py:22
  9.7 9.3 %collective-permute-start.1 = (f32[2,1,64,256]{3,2,1,0:T(8,128)}, f32[2,1,64,256]{3,2,1,0:T(8,128)S(1)}, u32[]{:S(2)}, u32[]{:S(2)}) collective-permute-start(f32[2,1,64,256]{3,2,1,0:T(8,128)} %get-tuple-element.66), channel_id=1, source_target_pairs={{1,0},{2,1},{3,2},{4,3},{5,4},{6,5},{7,6},{8,7},{9,8},{10,9},{11,1... | collective-permute-start | bytes 393224 | tf_op jit(solution)/shard_map/ppermute | solution.py:34
  15.4 6.0 %collective-permute-start.2 = (f32[2,1,64,256]{3,2,1,0:T(8,128)S(1)}, f32[2,1,64,256]{3,2,1,0:T(8,128)S(1)}, u32[]{:S(2)}, u32[]{:S(2)}) collective-permute-start(f32[2,1,64,256]{3,2,1,0:T(8,128)S(1)} %get-tuple-element.67), channel_id=1, source_target_pairs={{0,1},{1,2},{2,3},{3,4},{4,5},{5,6},{6,7},{7,8},{8,9},{9,10},{10,1... | collective-permute-start | bytes 393224 | tf_op jit(solution)/shard_map/ppermute | solution.py:31
  17.9 1.0 copy-start.6
  17.9 3.5 %copy-start.4 = (f32[2,8,64,1]{3,2,1,0:T(8,128)S(1)}, f32[2,8,64,1]{3,2,1,0:T(8,128)}, u32[]{:S(2)}) copy-start(f32[2,8,64,1]{3,2,1,0:T(8,128)} %get-tuple-element.58) | copy-start | bytes 12292
  17.9 3.5 %copy-start.5 = (f32[2,8,64,1]{3,2,1,0:T(8,128)S(1)}, f32[2,8,64,1]{3,2,1,0:T(8,128)}, u32[]{:S(2)}) copy-start(f32[2,8,64,1]{3,2,1,0:T(8,128)} %get-tuple-element.59) | copy-start | bytes 12292
  18.1 3.3 %copy-start.2 = (f32[2,8,64,255]{3,2,1,0:T(8,128)S(1)}, f32[2,8,64,255]{3,2,1,0:T(8,128)}, u32[]{:S(2)}) copy-start(f32[2,8,64,255]{3,2,1,0:T(8,128)} %get-tuple-element.57) | copy-start | bytes 3133444
  18.2 3.3 %copy-start.3 = (f32[1,8,64,256]{3,2,1,0:T(8,128)S(1)}, f32[1,8,64,256]{3,2,1,0:T(8,128)}, u32[]{:S(2)}) copy-start(f32[1,8,64,256]{3,2,1,0:T(8,128)} %get-tuple-element.65) | copy-start | bytes 1572868
  22.5 1.8 %copy-start.1 = (f32[2,8,64,256]{3,2,1,0:T(8,128)}, f32[2,8,64,256]{3,2,1,0:T(8,128)S(1)}, u32[]{:S(2)}) copy-start(f32[2,8,64,256]{3,2,1,0:T(8,128)S(1)} %fusion.29) | copy-start | bytes 3145732
  24.3 24.1 %all-to-all-start = ((f32[2,512,256]{2,0,1:T(2,128)}), f32[2,512,256]{2,0,1:T(2,128)S(1)}, u32[]{:S(2)}, u32[]{:S(2)}) async-start(f32[2,512,256]{2,0,1:T(2,128)} %bitcast.47), calls=%async_computation | async-start | bytes 2097152 | tf_op jit(solution)/shard_map/all_to_all | solution.py:114
  73.5 17.2 %collective-permute-start.3 = (f32[1,2,5,64,256]{4,3,2,1,0:T(8,128)}, f32[1,2,5,64,256]{4,3,2,1,0:T(8,128)S(1)}, u32[]{:S(2)}, u32[]{:S(2)}) collective-permute-start(f32[1,2,5,64,256]{4,3,2,1,0:T(8,128)} %get-tuple-element.54), channel_id=1, source_target_pairs={{0,1},{1,2},{2,3},{3,4},{4,5},{5,6},{6,7},{7,8},{8,9},{9,10},{10,1... | collective-permute-start | bytes 1966088 | tf_op jit(solution)/shard_map/ppermute | solution.py:31
  73.5 17.2 %collective-permute-start.4 = (f32[1,2,5,64,256]{4,3,2,1,0:T(8,128)S(1)}, f32[1,2,5,64,256]{4,3,2,1,0:T(8,128)}, u32[]{:S(2)}, u32[]{:S(2)}) collective-permute-start(f32[1,2,5,64,256]{4,3,2,1,0:T(8,128)S(1)} %get-tuple-element.55), channel_id=1, source_target_pairs={{1,0},{2,1},{3,2},{4,3},{5,4},{6,5},{7,6},{8,7},{9,8},{10,9},{11,1... | collective-permute-start | bytes 1966088 | tf_op jit(solution)/shard_map/ppermute | solution.py:34
  110.5 23.5 %all-to-all-start.2 = ((f32[2,512,256]{2,0,1:T(2,128)}), f32[2,512,256]{2,0,1:T(2,128)S(1)}, u32[]{:S(2)}, u32[]{:S(2)}) async-start(f32[2,512,256]{2,0,1:T(2,128)} %copy.23), calls=%async_computation.2 | async-start | bytes 2097152 | tf_op jit(solution)/shard_map/all_to_all | solution.py:145
where the time goes:
time: 160 us; the launch traced here: 159 us
  waiting for transfers between devices  50.2 us (31%)
  blocking collectives  41.2 us (26%)
  starting transfers between devices  28.7 us (18%)
  local copies, waits for them, and re-layouts  21.8 us (14%)
  other arithmetic  13.7 us (9%)
  matrix products  2.24 us (1%)
    all_to_all x1, blocking collectives, body(): lax.all_to_all(spectra, 'tm', split_axis=0, concat_axis=1, tiled=True)  20.6 us
    all_to_all x1, blocking collectives, body(): lax.all_to_all(restored, 'tm', split_axis=0, concat_axis=1, tiled=True)  20.6 us
    all_to_all x1, waiting for transfers between devices, body(): lax.all_to_all(solved_rows, 'tm', split_axis=1, concat_axis=0, tiled=True)  17.2 us
    all_to_all x1, waiting for transfers between devices, body(): lax.all_to_all(flattened, 'tm', split_axis=1, concat_axis=0, tiled=True)  17.2 us
    ppermute x2, waiting for transfers between devices, extended(): lax.ppermute(lax.slice_in_dim(block, block.shape[dim] - width, None, axis...  15.8 us
    ppermute x2, starting transfers between devices, extended(): lax.ppermute(lax.slice_in_dim(block, 0, width, axis=dim), axis, backward)  9.26 us
    add x5, other arithmetic, body(): source + nearby  6.92 us
    all_to_all x1, starting transfers between devices, body(): lax.all_to_all(flattened, 'tm', split_axis=1, concat_axis=0, tiled=True)  6.91 us
  transfers between devices with their start and end apart: 7, of which 4 were waited for; matrix products, arithmetic and copies ran while one was open for 2% of the time, Pallas kernels for 0%

commit v1 on v0

v1 whole, which is shorter than its diff:
```python
import math

import jax
import jax.numpy as jnp
import ml_dtypes
import numpy as np
from jax import lax
from jax.experimental import pallas as pl
from jax.experimental.pallas import tpu as pltpu
from jax.sharding import PartitionSpec as P

MESH = pl.DeviceIdType.MESH
SWEEPS = 6
STEPS, NX, NY, NZ = 32, 128, 64, 256
ROWS = 16
RING = 16
SLAB = NX // RING
REACH = SWEEPS - 1
WIDE = SLAB + 2 * REACH
SUB, LANE = 8, 128
CHUNKS = 2

alpha_value = 0.1
time_step = 0.1
couple_first = 0.4
couple_cross = 0.05
reaction_shift = 0.1
relaxation = 0.9
rho = alpha_value ** (1.0 / STEPS)


def real_basis(n):
    cells = np.arange(n)
    rows, freq = np.zeros((n, n)), np.zeros(n)
    rows[0] = 1.0 / math.sqrt(n)
    rows[1] = (-1.0) ** cells / math.sqrt(n)
    freq[1] = n // 2
    for k in range(1, n // 2):
        angle = 2.0 * math.pi * (k * cells % n) / n
        rows[2 * k] = math.sqrt(2.0 / n) * np.cos(angle)
        rows[2 * k + 1] = math.sqrt(2.0 / n) * np.sin(angle)
        freq[2 * k] = freq[2 * k + 1] = k
    return rows, freq


def halves(matrix):
    high = matrix.astype(ml_dtypes.bfloat16)
    low = (matrix - high.astype(np.float64)).astype(ml_dtypes.bfloat16)
    return high, low


def mode_factors(k):
    theta = 2.0 * math.pi * k / STEPS
    diag = 1.0 + reaction_shift + 2.0 * couple_first + 4.0 * couple_cross
    shift = complex(diag - rho * math.cos(theta), rho * math.sin(theta))
    scale = relaxation / shift
    beta = couple_first * scale
    roots = [complex(np.exp(2j * math.pi * j / SWEEPS)) for j in range(1, SWEEPS)]
    return [(1.0 - relaxation - root) / beta for root in roots], beta**REACH * scale


def constants():
    basis_z, freq_z = real_basis(NZ)
    basis_y, freq_y = real_basis(NY)
    wave_z = 2.0 * np.cos(2.0 * math.pi * freq_z / NZ)
    wave_y = 2.0 * np.cos(2.0 * math.pi * freq_y / NY)
    mu = (couple_cross / couple_first) * (wave_y[:, None] + wave_z[None, :])
    mu = mu.reshape(NY // SUB, SUB, NZ // LANE, LANE).transpose(0, 2, 1, 3)
    mu = mu.reshape(ROWS, SUB, LANE).astype(np.float32)
    zf = np.stack(halves(basis_z.T))
    zb = np.stack(halves(basis_z))
    yh, yl = halves(basis_y)
    yf = np.concatenate([yh, yh, yl], axis=1)
    yh, yl = halves(basis_y.T)
    yb = np.concatenate([yh, yh, yl], axis=1)
    table = []
    for k in range(1, STEPS // 2):
        factors, last = mode_factors(k)
        for value in factors + [last]:
            table += [value.real, value.imag]
    return mu, zf, zb, np.stack([yf, yb]), np.asarray(table, np.float32)


def split(value):
    high = value.astype(jnp.bfloat16)
    low = (value - high.astype(jnp.float32)).astype(jnp.bfloat16)
    return high, low


def dot(a, b):
    return jnp.dot(a, b, preferred_element_type=jnp.float32)


def rfft(x):
    n = len(x)
    if n == 2:
        return [(x[0] + x[1], None), (x[0] - x[1], None)]
    even, odd = rfft(x[0::2]), rfft(x[1::2])
    h, q = n // 2, n // 4
    out = [None] * (h + 1)
    out[0] = (even[0][0] + odd[0][0], None)
    out[h] = (even[0][0] - odd[0][0], None)
    out[q] = (even[q][0], -odd[q][0])
    for k in range(1, q):
        c, s = math.cos(2.0 * math.pi * k / n), -math.sin(2.0 * math.pi * k / n)
        er, ei = even[k]
        pr, pi = odd[k]
        tr, ti = c * pr - s * pi, c * pi + s * pr
        out[k] = (er + tr, ei + ti)
        out[h - k] = (er - tr, ti - ei)
    return out


def irfft(modes):
    n = 2 * (len(modes) - 1)
    if n == 2:
        return [modes[0][0] + modes[1][0], modes[0][0] - modes[1][0]]
    h, q = n // 2, n // 4
    even, odd = [None] * (q + 1), [None] * (q + 1)
    even[0] = (modes[0][0] + modes[h][0], None)
    odd[0] = (modes[0][0] - modes[h][0], None)
    even[q] = (2.0 * modes[q][0], None)
    odd[q] = (-2.0 * modes[q][1], None)
    for k in range(1, q):
        c, s = math.cos(2.0 * math.pi * k / n), math.sin(2.0 * math.pi * k / n)
        ar, ai = modes[k]
        br, bi = modes[h - k]
        even[k] = (ar + br, ai - bi)
        dr, di = ar - br, ai + bi
        odd[k] = (c * dr - s * di, c * di + s * dr)
    out = [None] * n
    out[0::2], out[1::2] = irfft(even), irfft(odd)
    return out


def kernel(
    state, initial, mu_ref, zf, zb, ymat, table,
    updated, residual,
    st, bef, res, upd, fore, mid, spec, back, ret, row_hi, row_lo,
    local_sem, edge_send, edge_recv, slab_send, slab_recv,
    fore_send, fore_recv, halo_send, halo_recv, back_send, back_recv,
):
    tm, sp = lax.axis_index("tm"), lax.axis_index("space")
    up, down = lax.rem(sp + 1, RING), lax.rem(sp + RING - 1, RING)

    def remote(src, dst, send, recv, device):
        return pltpu.make_async_remote_copy(
            src_ref=src, dst_ref=dst, send_sem=send, recv_sem=recv,
            device_id=device, device_id_type=MESH,
        )

    barrier = pltpu.get_barrier_semaphore()
    pl.semaphore_signal(barrier, inc=1, device_id=(tm, up), device_id_type=MESH)
    pl.semaphore_signal(barrier, inc=1, device_id=(tm, down), device_id_type=MESH)
    for o in range(1, ROWS):
        pl.semaphore_signal(
            barrier, inc=1, device_id=(jnp.bitwise_xor(tm, o), sp), device_id_type=MESH
        )
    load = pltpu.make_async_copy(state, st.at[:, pl.ds(1, SLAB)], local_sem.at[0])
    load.start()
    load.wait()

    @pl.when(tm == 0)
    def _():
        first = pltpu.make_async_copy(initial, bef, local_sem.at[1])
        first.start()
        first.wait()

    pl.semaphore_wait(barrier, ROWS + 1)

    edges = [
        remote(st.at[:, SLAB], st.at[:, 0], edge_send.at[0], edge_recv.at[0], (tm, up)),
        remote(st.at[:, 1], st.at[:, SLAB + 1], edge_send.at[1], edge_recv.at[1], (tm, down)),
    ]
    for copy in edges:
        copy.start()
    slab = remote(
        st.at[1, pl.ds(1, SLAB)], bef, slab_send.at[0], slab_recv.at[0],
        (lax.rem(tm + 1, ROWS), sp),
    )

    @pl.when(tm < ROWS - 1)
    def _():
        slab.start()

    def own_part(step, x):
        s = st[step, x + 1]
        near = st[step, x] + st[step, x + 2]
        cross = (
            pltpu.roll(s, 1, 0) + pltpu.roll(s, NY - 1, 0)
            + pltpu.roll(s, 1, 1) + pltpu.roll(s, NZ - 1, 1)
        )
        laplace = couple_first * (near - 2.0 * s) + couple_cross * (cross - 4.0 * s)
        return laplace - s + time_step * (s - s * s * s)

    def along_y(which, value):
        high, low = split(value)
        return dot(ymat[which], jnp.concatenate([high, low, high], axis=0))

    def keep_rows(at, value):
        high, low = split(value)
        rows = pl.ds(pl.multiple_of(at * NY, NY), NY)
        row_hi[rows] = high
        row_lo[rows] = low

    def along_z(matrix):
        high = row_hi[...]
        return dot(high, matrix[0]) + dot(row_lo[...], matrix[0]) + dot(high, matrix[1])

    def transform(step):
        gamma = jnp.exp(
            jnp.full((SUB, LANE), (2 * tm + step).astype(jnp.float32) * (math.log(alpha_value) / STEPS))
        )
        rows = along_z(zf)
        for x in range(SLAB):
            for g in range(ROWS):
                r0, c0 = x * NY + (g // 2) * SUB, (g % 2) * LANE
                fore[g, step, x] = rows[r0 : r0 + SUB, c0 : c0 + LANE] * gamma

    def fore_copy(step, o):
        peer = jnp.bitwise_xor(tm, o)
        return peer, remote(
            fore.at[peer, step], mid.at[step, tm, pl.ds(REACH, SLAB)],
            fore_send.at[step, o], fore_recv.at[step, o], (peer, sp),
        )

    def send_fore(step):
        @pl.loop(1, ROWS)
        def _(o):
            fore_copy(step, o)[1].start()

        own = pltpu.make_async_copy(
            fore.at[tm, step], mid.at[step, tm, pl.ds(REACH, SLAB)], local_sem.at[2 + step]
        )
        own.start()
        return own

    @pl.loop(1, SLAB - 1)
    def _(x):
        value = own_part(1, x) + st[0, x + 1]
        res[1, x] = value
        keep_rows(x, along_y(0, value))

    for copy in edges:
        copy.wait_recv()
    for x in (0, SLAB - 1):
        value = own_part(1, x) + st[0, x + 1]
        res[1, x] = value
        keep_rows(x, along_y(0, value))
    transform(1)
    own_odd = send_fore(1)

    @pl.loop(0, SLAB)
    def _(x):
        res[0, x] = own_part(0, x)

    @pl.when(tm > 0)
    def _():
        slab.wait_recv()

    @pl.loop(0, SLAB)
    def _(x):
        value = res[0, x] + bef[x]
        res[0, x] = value
        keep_rows(x, along_y(0, value))

    transform(0)
    own_even = send_fore(0)
    out_res = pltpu.make_async_copy(res, residual, local_sem.at[4])
    out_res.start()

    def halo_copies(step):
        return [
            remote(
                mid.at[step, :, pl.ds(SLAB, REACH)], mid.at[step, :, pl.ds(0, REACH)],
                halo_send.at[step, 0], halo_recv.at[step, 0], (tm, up),
            ),
            remote(
                mid.at[step, :, pl.ds(REACH, REACH)], mid.at[step, :, pl.ds(REACH + SLAB, REACH)],
                halo_send.at[step, 1], halo_recv.at[step, 1], (tm, down),
            ),
        ]

    for step, own in ((1, own_odd), (0, own_even)):
        own.wait()

        @pl.loop(1, ROWS)
        def _(o):
            peer = jnp.bitwise_xor(tm, o)
            landing = mid.at[step, peer, pl.ds(REACH, SLAB)]
            remote(
                landing, landing, fore_send.at[step, o], fore_recv.at[step, o], (peer, sp)
            ).wait_recv()

        for copy in halo_copies(step):
            copy.start()

    def to_modes(x):
        modes = rfft([mid[n % 2, n // 2, x] for n in range(STEPS)])
        spec[0, x] = modes[0][0]
        spec[1, x] = modes[STEPS // 2][0]
        for k in range(1, STEPS // 2):
            spec[2 * k, x] = modes[k][0]
            spec[2 * k + 1, x] = modes[k][1]

    @pl.loop(REACH, REACH + SLAB)
    def _(x):
        to_modes(x)

    for step in (1, 0):
        for copy in halo_copies(step):
            copy.wait_recv()

    @pl.loop(0, REACH)
    def _(x):
        to_modes(x)

    @pl.loop(REACH + SLAB, WIDE)
    def _(x):
        to_modes(x)

    mu = mu_ref[tm]

    for slot, k in ((0, 0), (1, STEPS // 2)):
        factors, last = mode_factors(k)
        v = [spec[slot, x] for x in range(WIDE)]
        for j in (0, 1):
            dr, square = mu + factors[j].real, factors[j].imag ** 2
            first = [v[x - 1] + v[x + 1] + dr * v[x] for x in range(1, len(v) - 1)]
            v = [
                first[x - 1] + first[x + 1] + dr * first[x] + square * v[x + 1]
                for x in range(1, len(first) - 1)
            ]
        dr = mu + factors[2].real
        v = [v[x - 1] + v[x + 1] + dr * v[x] for x in range(1, len(v) - 1)]
        for x in range(SLAB):
            spec[slot, x] = last.real * v[x]

    @pl.loop(1, STEPS // 2)
    def _(k):
        base = (k - 1) * 2 * SWEEPS
        vr = [spec[2 * k, x] for x in range(WIDE)]
        vi = [spec[2 * k + 1, x] for x in range(WIDE)]
        for j in range(REACH):
            dr, di = mu + table[base + 2 * j], table[base + 2 * j + 1]
            inner = range(1, len(vr) - 1)
            vr, vi = (
                [vr[x - 1] + vr[x + 1] + dr * vr[x] - di * vi[x] for x in inner],
                [vi[x - 1] + vi[x + 1] + dr * vi[x] + di * vr[x] for x in inner],
            )
        lr, li = table[base + 2 * REACH], table[base + 2 * REACH + 1]
        for x in range(SLAB):
            spec[2 * k, x] = lr * vr[x] - li * vi[x]
            spec[2 * k + 1, x] = lr * vi[x] + li * vr[x]

    part = SLAB // CHUNKS

    def back_copy(chunk, o):
        peer = jnp.bitwise_xor(tm, o)
        xs = pl.ds(chunk * part, part)
        return remote(
            back.at[peer, :, xs], ret.at[tm, :, xs],
            back_send.at[chunk, o], back_recv.at[chunk, o], (peer, sp),
        )

    own_back = []
    for chunk in range(CHUNKS):
        @pl.loop(chunk * part, (chunk + 1) * part)
        def _(x):
            modes = [(spec[0, x], None)]
            modes += [(spec[2 * k, x], spec[2 * k + 1, x]) for k in range(1, STEPS // 2)]
            modes += [(spec[1, x], None)]
            values = irfft(modes)
            for n in range(STEPS):
                back[n // 2, n % 2, x] = values[n]

        @pl.loop(1, ROWS)
        def _(o):
            back_copy(chunk, o).start()

        xs = pl.ds(chunk * part, part)
        own = pltpu.make_async_copy(
            back.at[tm, :, xs], ret.at[tm, :, xs], local_sem.at[5 + chunk]
        )
        own.start()
        own_back.append(own)

    out_upd = []
    planes = 2 * part
    for chunk in range(CHUNKS):
        own_back[chunk].wait()
        xs = pl.ds(chunk * part, part)

        @pl.loop(1, ROWS)
        def _(o):
            peer = jnp.bitwise_xor(tm, o)
            landing = ret.at[peer, :, xs]
            remote(
                landing, landing, back_send.at[chunk, o], back_recv.at[chunk, o], (peer, sp)
            ).wait_recv()

        for at in range(planes):
            step, x = at // part, chunk * part + at % part
            for pair in range(NY // (2 * SUB)):
                tiles = [
                    jnp.concatenate([ret[4 * pair + 2 * i, step, x], ret[4 * pair + 2 * i + 1, step, x]], axis=1)
                    for i in (0, 1)
                ]
                high, low = split(jnp.concatenate(tiles, axis=0))
                rows = pl.ds(at * NY + pair * 2 * SUB, 2 * SUB)
                row_hi[rows] = high
                row_lo[rows] = low
        high, low = row_hi[pl.ds(0, planes * NY)], row_lo[pl.ds(0, planes * NY)]
        value = dot(high, zb[0]) + dot(low, zb[0]) + dot(high, zb[1])
        for at in range(planes):
            step, x = at // part, chunk * part + at % part
            scale = jnp.exp(
                jnp.full(
                    (SUB, LANE),
                    (2 * tm + step).astype(jnp.float32) * (-math.log(alpha_value) / STEPS) - math.log(STEPS),
                )
            )
            delta = along_y(1, value[at * NY : (at + 1) * NY])
            upd[step, x] = st[step, x + 1] + delta * jnp.tile(scale, (NY // SUB, NZ // LANE))
        copy = pltpu.make_async_copy(upd.at[:, xs], updated.at[:, xs], local_sem.at[7 + chunk])
        copy.start()
        out_upd.append(copy)

    for copy in edges:
        copy.wait_send()

    @pl.when(tm < ROWS - 1)
    def _():
        slab.wait_send()

    for step in (1, 0):
        for copy in halo_copies(step):
            copy.wait_send()

    @pl.loop(1, ROWS)
    def _(o):
        for step in (1, 0):
            fore_copy(step, o)[1].wait_send()
        for chunk in range(CHUNKS):
            back_copy(chunk, o).wait_send()

    out_res.wait()
    for copy in out_upd:
        copy.wait()


def body(state, initial):
    mu, zf, zb, ymat, table = (jnp.asarray(c) for c in constants())
    whole = jax.ShapeDtypeStruct(state.shape, jnp.float32)
    steps = STEPS // ROWS
    vmem = pl.BlockSpec(memory_space=pltpu.VMEM)
    anywhere = pl.BlockSpec(memory_space=pl.ANY)
    f32 = jnp.float32
    return pl.pallas_call(
        kernel,
        out_shape=(whole, whole),
        in_specs=[anywhere, anywhere, vmem, vmem, vmem, vmem, pl.BlockSpec(memory_space=pltpu.SMEM)],
        out_specs=(anywhere, anywhere),
        scratch_shapes=[
            pltpu.VMEM((steps, SLAB + 2, NY, NZ), f32),
            pltpu.VMEM((SLAB, NY, NZ), f32),
            pltpu.VMEM((steps, SLAB, NY, NZ), f32),
            pltpu.VMEM((steps, SLAB, NY, NZ), f32),
            pltpu.VMEM((ROWS, steps, SLAB, SUB, LANE), f32),
            pltpu.VMEM((steps, ROWS, WIDE, SUB, LANE), f32),
            pltpu.VMEM((STEPS, WIDE, SUB, LANE), f32),
            pltpu.VMEM((ROWS, steps, SLAB, SUB, LANE), f32),
            pltpu.VMEM((ROWS, steps, SLAB, SUB, LANE), f32),
            pltpu.VMEM((SLAB * NY, NZ), jnp.bfloat16),
            pltpu.VMEM((SLAB * NY, NZ), jnp.bfloat16),
            pltpu.SemaphoreType.DMA((7 + CHUNKS,)),
            pltpu.SemaphoreType.DMA((2,)),
            pltpu.SemaphoreType.DMA((2,)),
            pltpu.SemaphoreType.DMA((1,)),
            pltpu.SemaphoreType.DMA((1,)),
            pltpu.SemaphoreType.DMA((steps, ROWS)),
            pltpu.SemaphoreType.DMA((steps, ROWS)),
            pltpu.SemaphoreType.DMA((steps, 2)),
            pltpu.SemaphoreType.DMA((steps, 2)),
            pltpu.SemaphoreType.DMA((CHUNKS, ROWS)),
            pltpu.SemaphoreType.DMA((CHUNKS, ROWS)),
        ],
        compiler_params=pltpu.CompilerParams(
            collective_id=0, has_side_effects=True, vmem_limit_bytes=40 * 2**20
        ),
        cost_estimate=pl.CostEstimate(flops=10**9, bytes_accessed=8 * 2**20, transcendentals=0),
    )(state, initial, mu, zf, zb, ymat, table)


def solution(mesh):
    in_specs = (P("tm", "space", None, None), P("space", None, None))
    out_specs = (P("tm", "space", None, None), P("tm", "space", None, None))
    return jax.shard_map(body, mesh=mesh, in_specs=in_specs, out_specs=out_specs, check_vma=False)
```

time: 160 us -> 91.5 us (0.57)
  the two profiles are of different devices: /device:TPU:1 before, /device:TPU:25 now
where the time goes in v1:
time: 91.5 us; the launch traced here: 91.1 us
  Pallas kernels  82 us (90%)
  local copies, waits for them, and re-layouts  8.46 us (9%)
    pallas_call x1, Pallas kernels, body(): pl.pallas_call(kernel, out_shape=(whole, whole), in_specs=[anywhere, anyw...  82 us
    unnamed x16, local copies, waits for them, and re-layouts  8.46 us

profile of v1, /device:TPU:25, one launch (start us, length us, event | category | flops | bytes accessed | tf_op | source)
XLA Modules:
  0.0 91.1 jit_solution(12690714754050483455)
XLA Ops:
  0.6 0.0 copy-start.6
  0.6 0.7 copy-done.6
  1.3 0.0 copy-start
  1.3 1.2 %copy-done = f32[2,8,64,256]{3,2,1,0:T(8,128)S(1)} copy-done((f32[2,8,64,256]{3,2,1,0:T(8,128)S(1)}, f32[2,8,64,256]{3,2,1,0:T(8,128)}, u32[]{:S(2)}) %copy-start) | copy-done | bytes 1048600
  2.5 0.0 copy-start.1
  2.5 1.0 %copy-done.1 = f32[8,64,256]{2,1,0:T(8,128)S(1)} copy-done((f32[8,64,256]{2,1,0:T(8,128)S(1)}, f32[8,64,256]{2,1,0:T(8,128)}, u32[]{:S(2)}) %copy-start.1) | copy-done | bytes 524312
  3.6 0.0 copy-start.2
  3.6 0.9 %copy-done.2 = bf16[2,256,256]{2,1,0:T(8,128)(2,1)S(1)} copy-done((bf16[2,256,256]{2,1,0:T(8,128)(2,1)S(1)}, bf16[2,256,256]{2,1,0:T(8,128)(2,1)}, u32[]{:S(2)}) %copy-start.2) | copy-done | bytes 262168
  4.5 0.0 copy-start.3
  4.5 0.9 %copy-done.3 = bf16[2,256,256]{2,1,0:T(8,128)(2,1)S(1)} copy-done((bf16[2,256,256]{2,1,0:T(8,128)(2,1)S(1)}, bf16[2,256,256]{2,1,0:T(8,128)(2,1)}, u32[]{:S(2)}) %copy-start.3) | copy-done | bytes 262168
  5.5 0.0 copy-start.4
  5.5 0.8 copy-done.4
  6.3 0.0 copy-start.5
  6.3 0.8 copy-done.5
  7.2 82.0 %shard_map.86 = (f32[2,8,64,256]{3,2,1,0:T(8,128)S(1)}, f32[2,8,64,256]{3,2,1,0:T(8,128)S(1)}) custom-call(f32[2,8,64,256]{3,2,1,0:T(8,128)S(1)} %copy-done, f32[8,64,256]{2,1,0:T(8,128)S(1)} %copy-done.1, f32[16,8,128]{2,1,0:T(8,128)S(1)} %copy-done.5, bf16[2,256,256]{2,1,0:T(8,128)(2,1)S(1)} %copy-done.3, bf16[2,256,256]{2,1,0:T(8,128)(2,1)S(1)} %copy-done.2, ...), custom_call_target="tpu_custom_call" | custom-call | flops 1000000000 | bytes 8388608 | tf_op jit(solution)/shard_map/pallas_call | solution.py:459
  89.2 1.0 %copy.11 = f32[2,8,64,256]{3,2,1,0:T(8,128)} copy(f32[2,8,64,256]{3,2,1,0:T(8,128)S(1)} %get-tuple-element.4) | data formatting | bytes 2097152
  90.2 1.0 %copy.12 = f32[2,8,64,256]{3,2,1,0:T(8,128)} copy(f32[2,8,64,256]{3,2,1,0:T(8,128)S(1)} %get-tuple-element.5) | data formatting | bytes 2097152
Async XLA Ops:
  0.6 0.7 copy-start.6
  1.3 1.2 %copy-start = (f32[2,8,64,256]{3,2,1,0:T(8,128)S(1)}, f32[2,8,64,256]{3,2,1,0:T(8,128)}, u32[]{:S(2)}) copy-start(f32[2,8,64,256]{3,2,1,0:T(8,128)} %state.1) | copy-start | bytes 3145732
  2.5 1.0 %copy-start.1 = (f32[8,64,256]{2,1,0:T(8,128)S(1)}, f32[8,64,256]{2,1,0:T(8,128)}, u32[]{:S(2)}) copy-start(f32[8,64,256]{2,1,0:T(8,128)} %initial.1) | copy-start | bytes 1572868
  3.6 0.9 %copy-start.2 = (bf16[2,256,256]{2,1,0:T(8,128)(2,1)S(1)}, bf16[2,256,256]{2,1,0:T(8,128)(2,1)}, u32[]{:S(2)}) copy-start(bf16[2,256,256]{2,1,0:T(8,128)(2,1)} %constant.12.clone.zb) | copy-start | bytes 786436
  4.5 0.9 %copy-start.3 = (bf16[2,256,256]{2,1,0:T(8,128)(2,1)S(1)}, bf16[2,256,256]{2,1,0:T(8,128)(2,1)}, u32[]{:S(2)}) copy-start(bf16[2,256,256]{2,1,0:T(8,128)(2,1)} %constant.11.clone.zf) | copy-start | bytes 786436
  5.5 0.8 copy-start.4
  6.3 0.8 copy-start.5

commit v2 on v1

--- a/solution.py
+++ b/solution.py
@@ -14,10 +14,14 @@
 STEPS, NX, NY, NZ = 32, 128, 64, 256
 ROWS = 16
 RING = 16
+PAIR, DEPTH = 2, 8
+GROUP = ROWS * PAIR
 SLAB = NX // RING
 REACH = SWEEPS - 1
 WIDE = SLAB + 2 * REACH
 SUB, LANE = 8, 128
+HALF = SUB // PAIR
+GAMMA = (STEPS // 2 - 1) * 2 * SWEEPS
 CHUNKS = 2
 
 alpha_value = 0.1
@@ -65,8 +69,8 @@
     wave_z = 2.0 * np.cos(2.0 * math.pi * freq_z / NZ)
     wave_y = 2.0 * np.cos(2.0 * math.pi * freq_y / NY)
     mu = (couple_cross / couple_first) * (wave_y[:, None] + wave_z[None, :])
-    mu = mu.reshape(NY // SUB, SUB, NZ // LANE, LANE).transpose(0, 2, 1, 3)
-    mu = mu.reshape(ROWS, SUB, LANE).astype(np.float32)
+    mu = mu.reshape(ROWS, HALF, PAIR, LANE).transpose(0, 2, 1, 3)
+    mu = np.tile(mu.reshape(GROUP, HALF, LANE), (1, PAIR, 1)).astype(np.float32)
     zf = np.stack(halves(basis_z.T))
     zb = np.stack(halves(basis_z))
     yh, yl = halves(basis_y)
@@ -78,6 +82,8 @@
         factors, last = mode_factors(k)
         for value in factors + [last]:
             table += [value.real, value.imag]
+    gamma = alpha_value ** (np.arange(STEPS) / STEPS)
+    table += list(gamma) + list(1.0 / (STEPS * gamma))
     return mu, zf, zb, np.stack([yf, yb]), np.asarray(table, np.float32)
 
 
@@ -134,14 +140,17 @@
 
 
 def kernel(
-    state, initial, mu_ref, zf, zb, ymat, table,
+    state, initial, mu_all, zf_all, zb_all, ymat_all, table_all,
     updated, residual,
-    st, bef, res, upd, fore, mid, spec, back, ret, row_hi, row_lo,
+    st, bef, res, upd, fore, mid, spec, back, ret, row_hi, row_lo, mu_ref, zf, zb, ymat, table,
     local_sem, edge_send, edge_recv, slab_send, slab_recv,
     fore_send, fore_recv, halo_send, halo_recv, back_send, back_recv,
 ):
     tm, sp = lax.axis_index("tm"), lax.axis_index("space")
+    pair, z = sp // DEPTH, lax.rem(sp, DEPTH)
     up, down = lax.rem(sp + 1, RING), lax.rem(sp + RING - 1, RING)
+    above = pair * DEPTH + lax.rem(z + 1, DEPTH)
+    below = pair * DEPTH + lax.rem(z + DEPTH - 1, DEPTH)
 
     def remote(src, dst, send, recv, device):
         return pltpu.make_async_remote_copy(
@@ -149,16 +158,28 @@
             device_id=device, device_id_type=MESH,
         )
 
+    def member(o):
+        t, p = jnp.bitwise_xor(tm, lax.rem(o, ROWS)), lax.rem(pair + o // ROWS, PAIR)
+        return t, p, (t, p * DEPTH + z)
+
     barrier = pltpu.get_barrier_semaphore()
-    pl.semaphore_signal(barrier, inc=1, device_id=(tm, up), device_id_type=MESH)
-    pl.semaphore_signal(barrier, inc=1, device_id=(tm, down), device_id_type=MESH)
-    for o in range(1, ROWS):
-        pl.semaphore_signal(
-            barrier, inc=1, device_id=(jnp.bitwise_xor(tm, o), sp), device_id_type=MESH
-        )
+    for near in (up, down, above, below):
+        pl.semaphore_signal(barrier, inc=1, device_id=(tm, near), device_id_type=MESH)
+
+    @pl.loop(1, GROUP)
+    def _(o):
+        pl.semaphore_signal(barrier, inc=1, device_id=member(o)[2], device_id_type=MESH)
+
     load = pltpu.make_async_copy(state, st.at[:, pl.ds(1, SLAB)], local_sem.at[0])
     load.start()
-    load.wait()
+    loads = [
+        pltpu.make_async_copy(src, dst, local_sem.at[7 + 2 * CHUNKS + i])
+        for i, (src, dst) in enumerate(
+            ((ymat_all, ymat), (zf_all, zf), (table_all, table), (mu_all, mu_ref), (zb_all, zb))
+        )
+    ]
+    for copy in loads:
+        copy.start()
 
     @pl.when(tm == 0)
     def _():
@@ -166,7 +187,10 @@
         first.start()
         first.wait()
 
-    pl.semaphore_wait(barrier, ROWS + 1)
+    load.wait()
+    for copy in loads:
+        copy.wait()
+    pl.semaphore_wait(barrier, GROUP + 3)
 
     edges = [
         remote(st.at[:, SLAB], st.at[:, 0], edge_send.at[0], edge_recv.at[0], (tm, up)),
@@ -208,29 +232,30 @@
         return dot(high, matrix[0]) + dot(row_lo[...], matrix[0]) + dot(high, matrix[1])
 
     def transform(step):
-        gamma = jnp.exp(
-            jnp.full((SUB, LANE), (2 * tm + step).astype(jnp.float32) * (math.log(alpha_value) / STEPS))
-        )
+        gamma = table[GAMMA + 2 * tm + step]
         rows = along_z(zf)
         for x in range(SLAB):
-            for g in range(ROWS):
-                r0, c0 = x * NY + (g // 2) * SUB, (g % 2) * LANE
-                fore[g, step, x] = rows[r0 : r0 + SUB, c0 : c0 + LANE] * gamma
+            for g in range(GROUP):
+                r0, c0 = x * NY + (g // PAIR) * HALF, (g % PAIR) * LANE
+                fore[g, step, x] = rows[r0 : r0 + HALF, c0 : c0 + LANE] * gamma
+
+    def landing_fore(step, t, p):
+        return mid.at[step, t, pl.ds(REACH, SLAB), pl.ds(pl.multiple_of(HALF * p, HALF), HALF)]
 
     def fore_copy(step, o):
-        peer = jnp.bitwise_xor(tm, o)
-        return peer, remote(
-            fore.at[peer, step], mid.at[step, tm, pl.ds(REACH, SLAB)],
-            fore_send.at[step, o], fore_recv.at[step, o], (peer, sp),
+        t, p, device = member(o)
+        return remote(
+            fore.at[t * PAIR + p, step], landing_fore(step, tm, pair),
+            fore_send.at[step, o], fore_recv.at[step, o], device,
         )
 
     def send_fore(step):
-        @pl.loop(1, ROWS)
+        @pl.loop(1, GROUP)
         def _(o):
-            fore_copy(step, o)[1].start()
+            fore_copy(step, o).start()
 
         own = pltpu.make_async_copy(
-            fore.at[tm, step], mid.at[step, tm, pl.ds(REACH, SLAB)], local_sem.at[2 + step]
+            fore.at[tm * PAIR + pair, step], landing_fore(step, tm, pair), local_sem.at[2 + step]
         )
         own.start()
         return own
@@ -273,35 +298,38 @@
         return [
             remote(
                 mid.at[step, :, pl.ds(SLAB, REACH)], mid.at[step, :, pl.ds(0, REACH)],
-                halo_send.at[step, 0], halo_recv.at[step, 0], (tm, up),
+                halo_send.at[step, 0], halo_recv.at[step, 0], (tm, above),
             ),
             remote(
                 mid.at[step, :, pl.ds(REACH, REACH)], mid.at[step, :, pl.ds(REACH + SLAB, REACH)],
-                halo_send.at[step, 1], halo_recv.at[step, 1], (tm, down),
+                halo_send.at[step, 1], halo_recv.at[step, 1], (tm, below),
             ),
         ]
 
     for step, own in ((1, own_odd), (0, own_even)):
         own.wait()
 
-        @pl.loop(1, ROWS)
+        @pl.loop(1, GROUP)
         def _(o):
-            peer = jnp.bitwise_xor(tm, o)
-            landing = mid.at[step, peer, pl.ds(REACH, SLAB)]
+            t, p, device = member(o)
+            landing = landing_fore(step, t, p)
             remote(
-                landing, landing, fore_send.at[step, o], fore_recv.at[step, o], (peer, sp)
+                landing, landing, fore_send.at[step, o], fore_recv.at[step, o], device
             ).wait_recv()
 
         for copy in halo_copies(step):
             copy.start()
 
-    def to_modes(x):
-        modes = rfft([mid[n % 2, n // 2, x] for n in range(STEPS)])
-        spec[0, x] = modes[0][0]
-        spec[1, x] = modes[STEPS // 2][0]
+    def to_modes(x, turned=None):
+        values = [mid[n % 2, n // 2, x] for n in range(STEPS)]
+        modes = rfft(values)
+        slots = [modes[0][0], modes[STEPS // 2][0]]
         for k in range(1, STEPS // 2):
-            spec[2 * k, x] = modes[k][0]
-            spec[2 * k + 1, x] = modes[k][1]
+            slots += [modes[k][0], modes[k][1]]
+        for slot, value in enumerate(slots):
+            if turned is not None:
+                value = jnp.where(turned, pltpu.roll(value, HALF, 0), value)
+            spec[slot, x] = value
 
     @pl.loop(REACH, REACH + SLAB)
     def _(x):
@@ -313,13 +341,13 @@
 
     @pl.loop(0, REACH)
     def _(x):
-        to_modes(x)
+        to_modes(x, z == 0)
 
     @pl.loop(REACH + SLAB, WIDE)
     def _(x):
-        to_modes(x)
-
-    mu = mu_ref[tm]
+        to_modes(x, z == DEPTH - 1)
+
+    mu = mu_ref[tm * PAIR + pair]
 
     for slot, k in ((0, 0), (1, STEPS // 2)):
         factors, last = mode_factors(k)
@@ -355,12 +383,15 @@
 
     part = SLAB // CHUNKS
 
+    def leaving(chunk, t, p):
+        xs = pl.ds(chunk * part, part)
+        return back.at[t, :, xs, pl.ds(pl.multiple_of(HALF * p, HALF), HALF)]
+
     def back_copy(chunk, o):
-        peer = jnp.bitwise_xor(tm, o)
-        xs = pl.ds(chunk * part, part)
+        t, p, device = member(o)
         return remote(
-            back.at[peer, :, xs], ret.at[tm, :, xs],
-            back_send.at[chunk, o], back_recv.at[chunk, o], (peer, sp),
+            leaving(chunk, t, p), ret.at[tm * PAIR + pair, :, pl.ds(chunk * part, part)],
+            back_send.at[chunk, o], back_recv.at[chunk, o], device,
         )
 
     own_back = []
@@ -374,13 +405,13 @@
             for n in range(STEPS):
                 back[n // 2, n % 2, x] = values[n]
 
-        @pl.loop(1, ROWS)
+        @pl.loop(1, GROUP)
         def _(o):
             back_copy(chunk, o).start()
 
-        xs = pl.ds(chunk * part, part)
         own = pltpu.make_async_copy(
-            back.at[tm, :, xs], ret.at[tm, :, xs], local_sem.at[5 + chunk]
+            leaving(chunk, tm, pair), ret.at[tm * PAIR + pair, :, pl.ds(chunk * part, part)],
+            local_sem.at[7 + chunk],
         )
         own.start()
         own_back.append(own)
@@ -391,38 +422,36 @@
         own_back[chunk].wait()
         xs = pl.ds(chunk * part, part)
 
-        @pl.loop(1, ROWS)
+        @pl.loop(1, GROUP)
         def _(o):
-            peer = jnp.bitwise_xor(tm, o)
-            landing = ret.at[peer, :, xs]
+            t, p, device = member(o)
+            landing = ret.at[t * PAIR + p, :, xs]
             remote(
-                landing, landing, back_send.at[chunk, o], back_recv.at[chunk, o], (peer, sp)
+                landing, landing, back_send.at[chunk, o], back_recv.at[chunk, o], device
             ).wait_recv()
 
         for at in range(planes):
             step, x = at // part, chunk * part + at % part
-            for pair in range(NY // (2 * SUB)):
+            for four in range(NY // (4 * HALF)):
                 tiles = [
-                    jnp.concatenate([ret[4 * pair + 2 * i, step, x], ret[4 * pair + 2 * i + 1, step, x]], axis=1)
-                    for i in (0, 1)
+                    jnp.concatenate(
+                        [ret[(4 * four + i) * PAIR + p, step, x] for p in range(PAIR)], axis=1
+                    )
+                    for i in range(4)
                 ]
                 high, low = split(jnp.concatenate(tiles, axis=0))
-                rows = pl.ds(at * NY + pair * 2 * SUB, 2 * SUB)
+                rows = pl.ds(at * NY + four * 4 * HALF, 4 * HALF)
                 row_hi[rows] = high
                 row_lo[rows] = low
         high, low = row_hi[pl.ds(0, planes * NY)], row_lo[pl.ds(0, planes * NY)]
         value = dot(high, zb[0]) + dot(low, zb[0]) + dot(high, zb[1])
         for at in range(planes):
             step, x = at // part, chunk * part + at % part
-            scale = jnp.exp(
-                jnp.full(
-                    (SUB, LANE),
-                    (2 * tm + step).astype(jnp.float32) * (-math.log(alpha_value) / STEPS) - math.log(STEPS),
-                )
-            )
             delta = along_y(1, value[at * NY : (at + 1) * NY])
-            upd[step, x] = st[step, x + 1] + delta * jnp.tile(scale, (NY // SUB, NZ // LANE))
-        copy = pltpu.make_async_copy(upd.at[:, xs], updated.at[:, xs], local_sem.at[7 + chunk])
+            upd[step, x] = st[step, x + 1] + table[GAMMA + STEPS + 2 * tm + step] * delta
+        copy = pltpu.make_async_copy(
+            upd.at[:, xs], updated.at[:, xs], local_sem.at[7 + CHUNKS + chunk]
+        )
         copy.start()
         out_upd.append(copy)
 
@@ -437,10 +466,10 @@
         for copy in halo_copies(step):
             copy.wait_send()
 
-    @pl.loop(1, ROWS)
+    @pl.loop(1, GROUP)
     def _(o):
         for step in (1, 0):
-            fore_copy(step, o)[1].wait_send()
+            fore_copy(step, o).wait_send()
         for chunk in range(CHUNKS):
             back_copy(chunk, o).wait_send()
 
@@ -453,40 +482,44 @@
     mu, zf, zb, ymat, table = (jnp.asarray(c) for c in constants())
     whole = jax.ShapeDtypeStruct(state.shape, jnp.float32)
     steps = STEPS // ROWS
-    vmem = pl.BlockSpec(memory_space=pltpu.VMEM)
-    anywhere = pl.BlockSpec(memory_space=pl.ANY)
+    hbm = pl.BlockSpec(memory_space=pltpu.HBM)
     f32 = jnp.float32
     return pl.pallas_call(
         kernel,
         out_shape=(whole, whole),
-        in_specs=[anywhere, anywhere, vmem, vmem, vmem, vmem, pl.BlockSpec(memory_space=pltpu.SMEM)],
-        out_specs=(anywhere, anywhere),
+        in_specs=[hbm] * 7,
+        out_specs=(hbm, hbm),
         scratch_shapes=[
             pltpu.VMEM((steps, SLAB + 2, NY, NZ), f32),
             pltpu.VMEM((SLAB, NY, NZ), f32),
             pltpu.VMEM((steps, SLAB, NY, NZ), f32),
             pltpu.VMEM((steps, SLAB, NY, NZ), f32),
-            pltpu.VMEM((ROWS, steps, SLAB, SUB, LANE), f32),
+            pltpu.VMEM((GROUP, steps, SLAB, HALF, LANE), f32),
             pltpu.VMEM((steps, ROWS, WIDE, SUB, LANE), f32),
             pltpu.VMEM((STEPS, WIDE, SUB, LANE), f32),
             pltpu.VMEM((ROWS, steps, SLAB, SUB, LANE), f32),
-            pltpu.VMEM((ROWS, steps, SLAB, SUB, LANE), f32),
+            pltpu.VMEM((GROUP, steps, SLAB, HALF, LANE), f32),
             pltpu.VMEM((SLAB * NY, NZ), jnp.bfloat16),
             pltpu.VMEM((SLAB * NY, NZ), jnp.bfloat16),
-            pltpu.SemaphoreType.DMA((7 + CHUNKS,)),
+            pltpu.VMEM(mu.shape, f32),
+            pltpu.VMEM(zf.shape, jnp.bfloat16),
+            pltpu.VMEM(zb.shape, jnp.bfloat16),
+            pltpu.VMEM(ymat.shape, jnp.bfloat16),
+            pltpu.SMEM(table.shape, f32),
+            pltpu.SemaphoreType.DMA((12 + 2 * CHUNKS,)),
             pltpu.SemaphoreType.DMA((2,)),
             pltpu.SemaphoreType.DMA((2,)),
             pltpu.SemaphoreType.DMA((1,)),
             pltpu.SemaphoreType.DMA((1,)),
-            pltpu.SemaphoreType.DMA((steps, ROWS)),
-            pltpu.SemaphoreType.DMA((steps, ROWS)),
+            pltpu.SemaphoreType.DMA((steps, GROUP)),
+            pltpu.SemaphoreType.DMA((steps, GROUP)),
             pltpu.SemaphoreType.DMA((steps, 2)),
             pltpu.SemaphoreType.DMA((steps, 2)),
-            pltpu.SemaphoreType.DMA((CHUNKS, ROWS)),
-            pltpu.SemaphoreType.DMA((CHUNKS, ROWS)),
+            pltpu.SemaphoreType.DMA((CHUNKS, GROUP)),
+            pltpu.SemaphoreType.DMA((CHUNKS, GROUP)),
         ],
         compiler_params=pltpu.CompilerParams(
-            collective_id=0, has_side_effects=True, vmem_limit_bytes=40 * 2**20
+            collective_id=0, has_side_effects=True, vmem_limit_bytes=60 * 2**20
         ),
         cost_estimate=pl.CostEstimate(flops=10**9, bytes_accessed=8 * 2**20, transcendentals=0),
     )(state, initial, mu, zf, zb, ymat, table)

time: 91.5 us -> 70.4 us (0.77)
  the two profiles are of different devices: /device:TPU:25 before, /device:TPU:1 now
where the time goes in v2:
time: 70.4 us; the launch traced here: 70.3 us
  Pallas kernels  66.3 us (94%)
  local copies, waits for them, and re-layouts  3.36 us (5%)
    pallas_call x1, Pallas kernels, body(): pl.pallas_call(kernel, out_shape=(whole, whole), in_specs=[hbm] * 7, out_...  66.3 us
    unnamed x4, local copies, waits for them, and re-layouts  3.36 us

profile of v2, /device:TPU:1, one launch (start us, length us, event | category | flops | bytes accessed | tf_op | source)
XLA Modules:
  0.0 70.3 jit_solution(3763081316645582808)
XLA Ops:
  0.6 66.3 %shard_map.86 = (f32[2,8,64,256]{3,2,1,0:T(8,128)}, f32[2,8,64,256]{3,2,1,0:T(8,128)}) custom-call(f32[2,8,64,256]{3,2,1,0:T(8,128)} %state.1, f32[8,64,256]{2,1,0:T(8,128)} %initial.1, f32[32,8,128]{2,1,0:T(8,128)} %constant.10.clone.mu_all, bf16[2,256,256]{2,1,0:T(8,128)(2,1)} %constant.11.clone.zf_all, bf16[2,256,256]{2,1,0:T(8,128)(2,1)} %constant.12.clone.zb_all, ...), custom_call_target="tpu_custom_call" | custom-call | flops 1000000000 | bytes 8388608 | tf_op jit(solution)/shard_map/pallas_call | solution.py:487
  66.9 0.0 copy-start
  66.9 2.4 %copy.11 = f32[2,8,64,256]{3,2,1,0:T(8,128)} copy(f32[2,8,64,256]{3,2,1,0:T(8,128)} %get-tuple-element.4) | data formatting | bytes 2097152
  69.3 0.0 copy-done
  69.3 1.0 %copy.12 = f32[2,8,64,256]{3,2,1,0:T(8,128)} copy(f32[2,8,64,256]{3,2,1,0:T(8,128)S(1)} %copy-done) | data formatting | bytes 2097152
Async XLA Ops:
  66.9 2.4 %copy-start = (f32[2,8,64,256]{3,2,1,0:T(8,128)S(1)}, f32[2,8,64,256]{3,2,1,0:T(8,128)}, u32[]{:S(2)}) copy-start(f32[2,8,64,256]{3,2,1,0:T(8,128)} %get-tuple-element.5) | copy-start | bytes 3145732

commit v3 on v2

v3 whole, which is shorter than its diff:
```python
import math

import jax
import jax.numpy as jnp
import ml_dtypes
import numpy as np
from jax import lax
from jax.experimental import pallas as pl
from jax.experimental.pallas import tpu as pltpu
from jax.sharding import PartitionSpec as P

MESH = pl.DeviceIdType.MESH
SWEEPS = 6
STEPS, NX, NY, NZ = 32, 128, 64, 256
ROWS = 16
RING = 16
PAIR, DEPTH = 2, 8
GROUP = ROWS * PAIR
SLAB = NX // RING
REACH = SWEEPS - 1
WIDE = SLAB + 2 * REACH
SUB, LANE = 8, 128
HALF = SUB // PAIR
REAL = (STEPS // 2 - 1) * 2 * SWEEPS
GAMMA = REAL + 2 * SWEEPS
CHUNKS = 2
OWN = SLAB // 2
BATCH = 2 * PAIR

alpha_value = 0.1
time_step = 0.1
couple_first = 0.4
couple_cross = 0.05
reaction_shift = 0.1
relaxation = 0.9
rho = alpha_value ** (1.0 / STEPS)


def real_basis(n):
    cells = np.arange(n)
    rows, freq = np.zeros((n, n)), np.zeros(n)
    rows[0] = 1.0 / math.sqrt(n)
    rows[1] = (-1.0) ** cells / math.sqrt(n)
    freq[1] = n // 2
    for k in range(1, n // 2):
        angle = 2.0 * math.pi * (k * cells % n) / n
        rows[2 * k] = math.sqrt(2.0 / n) * np.cos(angle)
        rows[2 * k + 1] = math.sqrt(2.0 / n) * np.sin(angle)
        freq[2 * k] = freq[2 * k + 1] = k
    return rows, freq


def halves(matrix):
    high = matrix.astype(ml_dtypes.bfloat16)
    low = (matrix - high.astype(np.float64)).astype(ml_dtypes.bfloat16)
    return high, low


def mode_factors(k):
    theta = 2.0 * math.pi * k / STEPS
    diag = 1.0 + reaction_shift + 2.0 * couple_first + 4.0 * couple_cross
    shift = complex(diag - rho * math.cos(theta), rho * math.sin(theta))
    scale = relaxation / shift
    beta = couple_first * scale
    roots = [complex(np.exp(2j * math.pi * j / SWEEPS)) for j in range(1, SWEEPS)]
    return [(1.0 - relaxation - root) / beta for root in roots], beta**REACH * scale


def constants():
    basis_z, freq_z = real_basis(NZ)
    basis_y, freq_y = real_basis(NY)
    wave_z = 2.0 * np.cos(2.0 * math.pi * freq_z / NZ)
    wave_y = 2.0 * np.cos(2.0 * math.pi * freq_y / NY)
    mu = (couple_cross / couple_first) * (wave_y[:, None] + wave_z[None, :])
    mu = mu.reshape(ROWS, HALF, PAIR, LANE).transpose(0, 2, 1, 3)
    mu = np.tile(mu.reshape(GROUP, HALF, LANE), (1, PAIR, 1)).astype(np.float32)
    zf = np.stack(halves(basis_z.T))
    zb = np.stack(halves(basis_z))
    yh, yl = halves(basis_y)
    yf = np.concatenate([yh, yh, yl], axis=1)
    yh, yl = halves(basis_y.T)
    yb = np.concatenate([yh, yh, yl], axis=1)
    table = []
    for k in range(1, STEPS // 2):
        factors, last = mode_factors(k)
        for value in factors + [last]:
            table += [value.real, value.imag]
    for k in (0, STEPS // 2):
        factors, last = mode_factors(k)
        for value in factors[:2]:
            table += [value.real, value.imag**2]
        table += [factors[2].real, last.real]
    gamma = alpha_value ** (np.arange(STEPS) / STEPS)
    table += list(gamma) + list(1.0 / (STEPS * gamma))
    return mu, zf, zb, np.stack([yf, yb]), np.asarray(table, np.float32)


def split(value):
    high = value.astype(jnp.bfloat16)
    low = (value - high.astype(jnp.float32)).astype(jnp.bfloat16)
    return high, low


def dot(a, b):
    return jnp.dot(a, b, preferred_element_type=jnp.float32)


def rfft(x):
    n = len(x)
    if n == 2:
        return [(x[0] + x[1], None), (x[0] - x[1], None)]
    even, odd = rfft(x[0::2]), rfft(x[1::2])
    h, q = n // 2, n // 4
    out = [None] * (h + 1)
    out[0] = (even[0][0] + odd[0][0], None)
    out[h] = (even[0][0] - odd[0][0], None)
    out[q] = (even[q][0], -odd[q][0])
    for k in range(1, q):
        c, s = math.cos(2.0 * math.pi * k / n), -math.sin(2.0 * math.pi * k / n)
        er, ei = even[k]
        pr, pi = odd[k]
        tr, ti = c * pr - s * pi, c * pi + s * pr
        out[k] = (er + tr, ei + ti)
        out[h - k] = (er - tr, ti - ei)
    return out


def irfft(modes):
    n = 2 * (len(modes) - 1)
    if n == 2:
        return [modes[0][0] + modes[1][0], modes[0][0] - modes[1][0]]
    h, q = n // 2, n // 4
    even, odd = [None] * (q + 1), [None] * (q + 1)
    even[0] = (modes[0][0] + modes[h][0], None)
    odd[0] = (modes[0][0] - modes[h][0], None)
    even[q] = (2.0 * modes[q][0], None)
    odd[q] = (-2.0 * modes[q][1], None)
    for k in range(1, q):
        c, s = math.cos(2.0 * math.pi * k / n), math.sin(2.0 * math.pi * k / n)
        ar, ai = modes[k]
        br, bi = modes[h - k]
        even[k] = (ar + br, ai - bi)
        dr, di = ar - br, ai + bi
        odd[k] = (c * dr - s * di, c * di + s * dr)
    out = [None] * n
    out[0::2], out[1::2] = irfft(even), irfft(odd)
    return out


def kernel(
    state, initial, mu_all, zf_all, zb_all, ymat_all, table_all,
    updated, residual,
    st, late, res, upd, fore, third, mid, mid3, spec, back, ret, mu_ref, zf, zb, ymat, table,
    load_sem, own_sem, out_sem, edge_send, edge_recv, slab_send, slab_recv,
    fore_send, fore_recv, third_send, third_recv, halo_send, halo_recv, back_send, back_recv,
):
    tm, sp = lax.axis_index("tm"), lax.axis_index("space")
    pair, z = sp // DEPTH, lax.rem(sp, DEPTH)
    up, down = lax.rem(sp + 1, RING), lax.rem(sp + RING - 1, RING)
    above = pair * DEPTH + lax.rem(z + 1, DEPTH)
    below = pair * DEPTH + lax.rem(z + DEPTH - 1, DEPTH)
    both = pl.ds(1, 2)

    def remote(src, dst, send, recv, device):
        return pltpu.make_async_remote_copy(
            src_ref=src, dst_ref=dst, send_sem=send, recv_sem=recv,
            device_id=device, device_id_type=MESH,
        )

    def member(o):
        bit = [lax.rem(o // 2**i, 2) for i in range(5)]
        t = jnp.bitwise_xor(tm, bit[0] + 8 * bit[2] + 2 * bit[3] + 4 * bit[4])
        p = lax.rem(pair + bit[1], PAIR)
        return t, p, (t, p * DEPTH + z)

    nears = (up, down, above, below)
    barrier = pltpu.get_barrier_semaphore()
    for near in nears:
        pl.semaphore_signal(barrier, inc=1, device_id=(tm, near), device_id_type=MESH)

    @pl.loop(1, GROUP)
    def _(o):
        pl.semaphore_signal(barrier, inc=1, device_id=member(o)[2], device_id_type=MESH)

    loads = [
        pltpu.make_async_copy(src, dst, load_sem.at[i])
        for i, (src, dst) in enumerate(
            (
                (state, st.at[both, pl.ds(1, SLAB)]), (ymat_all, ymat), (zf_all, zf),
                (table_all, table), (mu_all, mu_ref), (zb_all, zb),
            )
        )
    ]
    for copy in loads:
        copy.start()

    @pl.when(tm == 0)
    def _():
        first = pltpu.make_async_copy(initial, st.at[0, pl.ds(1, SLAB)], own_sem.at[0])
        first.start()
        first.wait()

    odd = lax.rem(tm, 2) == 1
    extra = jnp.logical_and(odd, tm < ROWS - 1)
    later = jnp.logical_and(jnp.logical_not(odd), tm > 0)

    @pl.when(later)
    def _():
        @pl.loop(0, SLAB)
        def _(x):
            st[0, x + 1] = jnp.zeros((NY, NZ), jnp.float32)

    for copy in loads:
        copy.wait()

    edges = [
        remote(st.at[both, SLAB], st.at[both, 0], edge_send.at[0], edge_recv.at[0], (tm, up)),
        remote(st.at[both, 1], st.at[both, SLAB + 1], edge_send.at[1], edge_recv.at[1], (tm, down)),
    ]
    slab, slab_later = (
        remote(
            st.at[2, pl.ds(1, SLAB)], to, slab_send.at[0], slab_recv.at[0],
            (lax.rem(tm + 1, ROWS), sp),
        )
        for to in (st.at[0, pl.ds(1, SLAB)], late)
    )
    pl.semaphore_wait(barrier, GROUP - 1 + len(nears))
    for copy in edges:
        copy.start()

    @pl.when(jnp.logical_not(odd))
    def _():
        slab.start()

    def residual_of(step, x):
        s = st[step + 1, x + 1]
        near = st[step + 1, x] + st[step + 1, x + 2]
        cross = (
            pltpu.roll(s, 1, 0) + pltpu.roll(s, NY - 1, 0)
            + pltpu.roll(s, 1, 1) + pltpu.roll(s, NZ - 1, 1)
        )
        laplace = couple_first * (near - 2.0 * s) + couple_cross * (cross - 4.0 * s)
        return st[step, x + 1] - s + laplace + time_step * (s - s * s * s)

    def along_y(which, value):
        high, low = split(value)
        return dot(ymat[which], jnp.concatenate([high, low, high], axis=0))

    def along_z(matrix, value):
        high, low = split(value)
        return dot(high, matrix[0]) + dot(low, matrix[0]) + dot(high, matrix[1])

    def part_of(p):
        return pl.ds(pl.multiple_of(HALF * p, HALF), HALF)

    own_places = pl.ds(0, SLAB)

    def landing_fore(step, t, p):
        return mid.at[step, t, own_places, part_of(p)]

    def own_fore(step):
        return pltpu.make_async_copy(
            fore.at[tm * PAIR + pair, step], landing_fore(step, tm, pair), own_sem.at[step]
        )

    def landing_third(t, p):
        return mid3.at[t // 2, :, part_of(p)]

    def own_third():
        return pltpu.make_async_copy(
            third.at[tm * PAIR + pair], landing_third(tm, pair), own_sem.at[2 + CHUNKS]
        )

    def lay_out(target, place, rows):
        for j in range(2):
            for g in range(GROUP):
                r0, c0 = j * NY + (g // PAIR) * HALF, (g % PAIR) * LANE
                target(g, place + j, rows[r0 : r0 + HALF, c0 : c0 + LANE])

    def work(step, place):
        rows = []
        for j in range(2):
            x = lax.rem(place + j + 1, SLAB)
            value = residual_of(step, x)
            res[step, x] = value
            rows.append(along_y(0, value))
        rows = along_z(zf, jnp.concatenate(rows, axis=0)) * table[GAMMA + 2 * tm + step]

        def put(g, at, value):
            fore[g, step, at] = value

        lay_out(put, place, rows)

    def work_third(place):
        rows = [along_y(0, st[2, lax.rem(place + j + 1, SLAB) + 1]) for j in range(2)]
        rows = along_z(zf, jnp.concatenate(rows, axis=0)) * table[GAMMA + 2 * tm + 2]

        def put(g, at, value):
            third[g, at] = value

        lay_out(put, place, rows)

    @pl.loop(0, OWN - 1)
    def _(i):
        work(1, 2 * i)

    @pl.when(extra)
    def _():
        @pl.loop(0, OWN)
        def _(i):
            work_third(2 * i)

        @pl.loop(1, GROUP)
        def _(o):
            t, p, device = member(o)
            remote(
                third.at[t * PAIR + p], landing_third(tm, pair),
                third_send.at[0], third_recv.at[tm // 2, pair], device,
            ).start()

        own_third().start()

    for copy in edges:
        copy.wait_recv()

    @pl.loop(OWN - 1, 2 * OWN)
    def _(i):
        step, place = 1 - i // OWN, 2 * lax.rem(i, OWN)

        @pl.when(jnp.logical_and(i == OWN, odd))
        def _():
            slab.wait_recv()

        work(step, place)

        @pl.when(lax.rem(i, OWN) == OWN - 1)
        def _():
            @pl.loop(1, GROUP)
            def _(o):
                t, p, device = member(o)
                remote(
                    fore.at[t * PAIR + p, step], landing_fore(step, tm, pair),
                    fore_send.at[step], fore_recv.at[step, o], device,
                ).start()

            own_fore(step).start()

    def halo_copies(step, times=pl.ds(0, ROWS)):
        return [
            remote(
                mid.at[step, times, pl.ds(at, count)], mid.at[step, times, pl.ds(to, count)],
                halo_send.at[step, way], halo_recv.at[step, way], (tm, near),
            )
            for way, near, at, to, count in (
                (0, above, SLAB - REACH - 1, SLAB, REACH),
                (1, below, 0, SLAB + REACH + 1, REACH - 1),
                (2, below, SLAB - 1, SLAB + REACH, 1),
            )
        ]

    @pl.loop(0, 2 * GROUP // BATCH)
    def _(i):
        step, o0 = 1 - i // (GROUP // BATCH), lax.rem(i, GROUP // BATCH) * BATCH

        @pl.when(o0 == 0)
        def _():
            own_fore(step).wait()

        @pl.loop(0, BATCH)
        def _(j):
            @pl.when(o0 + j > 0)
            def _():
                t, p, device = member(o0 + j)
                landing = landing_fore(step, t, p)
                remote(
                    landing, landing, fore_send.at[step], fore_recv.at[step, o0 + j], device
                ).wait_recv()

        chip = member(o0)[0] // 2

        @pl.when(jnp.logical_and(step == 0, chip > 0))
        def _():
            for p in range(PAIR):
                source = 2 * chip - 1
                own = jnp.logical_and(tm == source, pair == p)

                @pl.when(own)
                def _():
                    own_third().wait()

                @pl.when(jnp.logical_not(own))
                def _():
                    landing = landing_third(source, p)
                    remote(
                        landing, landing, third_send.at[0], third_recv.at[source // 2, p],
                        (source, p * DEPTH + z),
                    ).wait_recv()

            mid[0, 2 * chip, own_places] = mid[0, 2 * chip, own_places] + mid3[chip - 1]

        for copy in halo_copies(step, pl.ds(2 * chip, 2)):
            copy.start()

    @pl.when(extra)
    def _():
        slab_later.start()

    @pl.loop(0, WIDE)
    def _(i):
        @pl.when(i == SLAB)
        def _():
            for step in (1, 0):
                for copy in halo_copies(step):
                    copy.wait_recv()

        before, after = jnp.logical_and(i >= SLAB, i < SLAB + REACH), i >= SLAB + REACH
        x = jnp.where(i < SLAB, REACH + lax.rem(i + 1, SLAB), jnp.where(before, i - SLAB, i))
        turned = jnp.logical_or(
            jnp.logical_and(before, z == 0), jnp.logical_and(after, z == DEPTH - 1)
        )
        modes = rfft([mid[n % 2, n // 2, i] for n in range(STEPS)])
        slots = [modes[0][0], modes[STEPS // 2][0]]
        for k in range(1, STEPS // 2):
            slots += [modes[k][0], modes[k][1]]
        for slot, value in enumerate(slots):
            spec[slot, x] = jnp.where(turned, pltpu.roll(value, HALF, 0), value)

    mu = mu_ref[tm * PAIR + pair]

    @pl.loop(0, 2)
    def _(slot):
        base = REAL + slot * SWEEPS
        v = [spec[slot, x] for x in range(WIDE)]
        for j in (0, 1):
            dr, square = mu + table[base + 2 * j], table[base + 2 * j + 1]
            first = [v[x - 1] + v[x + 1] + dr * v[x] for x in range(1, len(v) - 1)]
            v = [
                first[x - 1] + first[x + 1] + dr * first[x] + square * v[x + 1]
                for x in range(1, len(first) - 1)
            ]
        dr = mu + table[base + 4]
        v = [v[x - 1] + v[x + 1] + dr * v[x] for x in range(1, len(v) - 1)]
        for x in range(SLAB):
            spec[slot, x] = table[base + 5] * v[x]

    @pl.loop(1, STEPS // 2)
    def _(k):
        base = (k - 1) * 2 * SWEEPS
        vr = [spec[2 * k, x] for x in range(WIDE)]
        vi = [spec[2 * k + 1, x] for x in range(WIDE)]
        for j in range(REACH):
            dr, di = mu + table[base + 2 * j], table[base + 2 * j + 1]
            inner = range(1, len(vr) - 1)
            vr, vi = (
                [vr[x - 1] + vr[x + 1] + dr * vr[x] - di * vi[x] for x in inner],
                [vi[x - 1] + vi[x + 1] + dr * vi[x] + di * vr[x] for x in inner],
            )
        lr, li = table[base + 2 * REACH], table[base + 2 * REACH + 1]
        for x in range(SLAB):
            spec[2 * k, x] = lr * vr[x] - li * vi[x]
            spec[2 * k + 1, x] = lr * vi[x] + li * vr[x]

    part = SLAB // CHUNKS

    def planes_of(chunk):
        return pl.ds(pl.multiple_of(chunk * part, part), part)

    def leaving(chunk, t, p):
        return back.at[t, :, planes_of(chunk), part_of(p)]

    def landing_back(chunk, t, p):
        return ret.at[t * PAIR + p, :, planes_of(chunk)]

    def own_back(chunk):
        return pltpu.make_async_copy(
            leaving(chunk, tm, pair), landing_back(chunk, tm, pair), own_sem.at[2 + chunk]
        )

    @pl.loop(0, CHUNKS)
    def _(chunk):
        @pl.loop(0, part)
        def _(i):
            x = chunk * part + i
            modes = [(spec[0, x], None)]
            modes += [(spec[2 * k, x], spec[2 * k + 1, x]) for k in range(1, STEPS // 2)]
            modes += [(spec[1, x], None)]
            values = irfft(modes)
            for n in range(STEPS):
                back[n // 2, n % 2, x] = values[n]

        @pl.loop(1, GROUP)
        def _(o):
            t, p, device = member(o)
            remote(
                leaving(chunk, t, p), landing_back(chunk, tm, pair),
                back_send.at[chunk], back_recv.at[chunk, o], device,
            ).start()

        own_back(chunk).start()

    @pl.when(later)
    def _():
        slab_later.wait_recv()

        @pl.loop(0, SLAB)
        def _(x):
            res[0, x] = res[0, x] + late[x]

    out_res = pltpu.make_async_copy(res, residual, out_sem.at[0])
    out_res.start()

    def out_upd(chunk):
        xs = planes_of(chunk)
        return pltpu.make_async_copy(upd.at[:, xs], updated.at[:, xs], out_sem.at[1 + chunk])

    @pl.loop(0, CHUNKS)
    def _(chunk):
        own_back(chunk).wait()

        @pl.loop(1, GROUP)
        def _(o):
            t, p, device = member(o)
            landing = landing_back(chunk, t, p)
            remote(
                landing, landing, back_send.at[chunk], back_recv.at[chunk, o], device
            ).wait_recv()

        @pl.loop(0, part)
        def _(i):
            step, x0 = i // (part // 2), chunk * part + 2 * lax.rem(i, part // 2)
            rows = []
            for j in range(2):
                for r in range(ROWS):
                    rows.append(
                        jnp.concatenate([ret[r * PAIR + p, step, x0 + j] for p in range(PAIR)], axis=1)
                    )
            value = along_z(zb, jnp.concatenate(rows, axis=0))
            scale = table[GAMMA + STEPS + 2 * tm + step]
            for j in range(2):
                delta = along_y(1, value[j * NY : (j + 1) * NY])
                upd[step, x0 + j] = st[step + 1, x0 + j + 1] + scale * delta

        out_upd(chunk).start()

    for copy in edges:
        copy.wait_send()

    @pl.when(tm < ROWS - 1)
    def _():
        slab.wait_send()

    others = pl.ds(0, GROUP - 1)

    @pl.when(extra)
    def _():
        sent = third.at[others]
        remote(sent, sent, third_send.at[0], third_recv.at[0, 0], (tm, above)).wait_send()

    for step in (1, 0):
        for copy in halo_copies(step):
            copy.wait_send()
        sent = fore.at[others, step]
        remote(sent, sent, fore_send.at[step], fore_recv.at[step, 0], (tm, above)).wait_send()
    for chunk in range(CHUNKS):
        sent = ret.at[others, :, planes_of(chunk)]
        remote(sent, sent, back_send.at[chunk], back_recv.at[chunk, 0], (tm, above)).wait_send()
        out_upd(chunk).wait()
    out_res.wait()


def body(state, initial):
    mu, zf, zb, ymat, table = (jnp.asarray(c) for c in constants())
    whole = jax.ShapeDtypeStruct(state.shape, jnp.float32)
    steps = STEPS // ROWS
    hbm = pl.BlockSpec(memory_space=pltpu.HBM)
    f32 = jnp.float32
    return pl.pallas_call(
        kernel,
        out_shape=(whole, whole),
        in_specs=[hbm] * 7,
        out_specs=(hbm, hbm),
        scratch_shapes=[
            pltpu.VMEM((steps + 1, SLAB + 2, NY, NZ), f32),
            pltpu.VMEM((SLAB, NY, NZ), f32),
            pltpu.VMEM((steps, SLAB, NY, NZ), f32),
            pltpu.VMEM((steps, SLAB, NY, NZ), f32),
            pltpu.VMEM((GROUP, steps, SLAB, HALF, LANE), f32),
            pltpu.VMEM((GROUP, SLAB, HALF, LANE), f32),
            pltpu.VMEM((steps, ROWS, WIDE, SUB, LANE), f32),
            pltpu.VMEM((ROWS // 2, SLAB, SUB, LANE), f32),
            pltpu.VMEM((STEPS, WIDE, SUB, LANE), f32),
            pltpu.VMEM((ROWS, steps, SLAB, SUB, LANE), f32),
            pltpu.VMEM((GROUP, steps, SLAB, HALF, LANE), f32),
            pltpu.VMEM(mu.shape, f32),
            pltpu.VMEM(zf.shape, jnp.bfloat16),
            pltpu.VMEM(zb.shape, jnp.bfloat16),
            pltpu.VMEM(ymat.shape, jnp.bfloat16),
            pltpu.SMEM(table.shape, f32),
            pltpu.SemaphoreType.DMA((6,)),
            pltpu.SemaphoreType.DMA((3 + CHUNKS,)),
            pltpu.SemaphoreType.DMA((1 + CHUNKS,)),
            pltpu.SemaphoreType.DMA((2,)),
            pltpu.SemaphoreType.DMA((2,)),
            pltpu.SemaphoreType.DMA((1,)),
            pltpu.SemaphoreType.DMA((1,)),
            pltpu.SemaphoreType.DMA((steps,)),
            pltpu.SemaphoreType.DMA((steps, GROUP)),
            pltpu.SemaphoreType.DMA((1,)),
            pltpu.SemaphoreType.DMA((ROWS // 2, PAIR)),
            pltpu.SemaphoreType.DMA((steps, 3)),
            pltpu.SemaphoreType.DMA((steps, 3)),
            pltpu.SemaphoreType.DMA((CHUNKS,)),
            pltpu.SemaphoreType.DMA((CHUNKS, GROUP)),
        ],
        compiler_params=pltpu.CompilerParams(
            collective_id=0, has_side_effects=True, vmem_limit_bytes=60 * 2**20
        ),
        cost_estimate=pl.CostEstimate(flops=10**9, bytes_accessed=8 * 2**20, transcendentals=0),
    )(state, initial, mu, zf, zb, ymat, table)


def solution(mesh):
    in_specs = (P("tm", "space", None, None), P("space", None, None))
    out_specs = (P("tm", "space", None, None), P("tm", "space", None, None))
    return jax.shard_map(body, mesh=mesh, in_specs=in_specs, out_specs=out_specs, check_vma=False)
```

time: 70.4 us -> 65.5 us (0.930)
  Pallas kernels: 66.3 us -> 61.4 us
    pallas_call x1, Pallas kernels: 66.3 us -> 61.4 us  [body(): pl.pallas_call(kernel, out_shape=(whole, whole), in_specs=[hbm] * 7, out_...]
where the time goes in v3:
time: 65.5 us; the launch traced here: 65.4 us
  Pallas kernels  61.4 us (94%)
  local copies, waits for them, and re-layouts  3.36 us (5%)
    pallas_call x1, Pallas kernels, body(): pl.pallas_call(kernel, out_shape=(whole, whole), in_specs=[hbm] * 7, out_...  61.4 us
    unnamed x4, local copies, waits for them, and re-layouts  3.36 us

profile of v3, /device:TPU:1, one launch (start us, length us, event | category | flops | bytes accessed | tf_op | source)
XLA Modules:
  0.0 65.4 jit_solution(581839381044661305)
XLA Ops:
  0.6 61.4 %shard_map.86 = (f32[2,8,64,256]{3,2,1,0:T(8,128)}, f32[2,8,64,256]{3,2,1,0:T(8,128)}) custom-call(f32[2,8,64,256]{3,2,1,0:T(8,128)} %state.1, f32[8,64,256]{2,1,0:T(8,128)} %initial.1, f32[32,8,128]{2,1,0:T(8,128)} %constant.10.clone.mu_all, bf16[2,256,256]{2,1,0:T(8,128)(2,1)} %constant.11.clone.zf_all, bf16[2,256,256]{2,1,0:T(8,128)(2,1)} %constant.12.clone.zb_all, ...), custom_call_target="tpu_custom_call" | custom-call | flops 1000000000 | bytes 8388608 | tf_op jit(solution)/shard_map/pallas_call | solution.py:577
  62.0 0.0 copy-start
  62.0 2.4 %copy.11 = f32[2,8,64,256]{3,2,1,0:T(8,128)} copy(f32[2,8,64,256]{3,2,1,0:T(8,128)} %get-tuple-element.4) | data formatting | bytes 2097152
  64.4 0.0 copy-done
  64.4 1.0 %copy.12 = f32[2,8,64,256]{3,2,1,0:T(8,128)} copy(f32[2,8,64,256]{3,2,1,0:T(8,128)S(1)} %copy-done) | data formatting | bytes 2097152
Async XLA Ops:
  62.0 2.4 %copy-start = (f32[2,8,64,256]{3,2,1,0:T(8,128)S(1)}, f32[2,8,64,256]{3,2,1,0:T(8,128)}, u32[]{:S(2)}) copy-start(f32[2,8,64,256]{3,2,1,0:T(8,128)} %get-tuple-element.5) | copy-start | bytes 3145732

commit v4 on v3

--- a/solution.py
+++ b/solution.py
@@ -25,6 +25,7 @@
 GAMMA = REAL + 2 * SWEEPS
 CHUNKS = 2
 OWN = SLAB // 2
+PHASES = ((1, 1, 0, SLAB - 2), (0, 1, 0, SLAB - 2), (0, 2, SLAB - 2, 2))
 BATCH = 2 * PAIR
 
 alpha_value = 0.1
@@ -253,22 +254,36 @@
     def part_of(p):
         return pl.ds(pl.multiple_of(HALF * p, HALF), HALF)
 
-    own_places = pl.ds(0, SLAB)
-
-    def landing_fore(step, t, p):
-        return mid.at[step, t, own_places, part_of(p)]
-
-    def own_fore(step):
+    def landing_fore(phase, t, p):
+        step, steps, place, places = PHASES[phase]
+        return mid.at[pl.ds(step, steps), t, pl.ds(place, places), part_of(p)]
+
+    def leaving_fore(phase, t, p):
+        step, steps, place, places = PHASES[phase]
+        return fore.at[t * PAIR + p, pl.ds(step, steps), pl.ds(place, places)]
+
+    def own_fore(phase):
         return pltpu.make_async_copy(
-            fore.at[tm * PAIR + pair, step], landing_fore(step, tm, pair), own_sem.at[step]
-        )
+            leaving_fore(phase, tm, pair), landing_fore(phase, tm, pair), own_sem.at[phase]
+        )
+
+    def send_fore(phase):
+        @pl.loop(1, GROUP)
+        def _(o):
+            t, p, device = member(o)
+            remote(
+                leaving_fore(phase, t, p), landing_fore(phase, tm, pair),
+                fore_send.at[phase], fore_recv.at[phase, o], device,
+            ).start()
+
+        own_fore(phase).start()
 
     def landing_third(t, p):
         return mid3.at[t // 2, :, part_of(p)]
 
     def own_third():
         return pltpu.make_async_copy(
-            third.at[tm * PAIR + pair], landing_third(tm, pair), own_sem.at[2 + CHUNKS]
+            third.at[tm * PAIR + pair], landing_third(tm, pair), own_sem.at[3 + CHUNKS]
         )
 
     def lay_out(target, place, rows):
@@ -304,6 +319,16 @@
     def _(i):
         work(1, 2 * i)
 
+    @pl.when(z == 0)
+    def _():
+        edges[0].wait_recv()
+
+    @pl.when(z == DEPTH - 1)
+    def _():
+        edges[1].wait_recv()
+
+    send_fore(0)
+
     @pl.when(extra)
     def _():
         @pl.loop(0, OWN)
@@ -320,86 +345,94 @@
 
         own_third().start()
 
-    for copy in edges:
-        copy.wait_recv()
-
-    @pl.loop(OWN - 1, 2 * OWN)
+    @pl.when(odd)
+    def _():
+        slab.wait_recv()
+
+    @pl.loop(0, OWN - 1)
     def _(i):
-        step, place = 1 - i // OWN, 2 * lax.rem(i, OWN)
-
-        @pl.when(jnp.logical_and(i == OWN, odd))
-        def _():
-            slab.wait_recv()
-
-        work(step, place)
-
-        @pl.when(lax.rem(i, OWN) == OWN - 1)
-        def _():
-            @pl.loop(1, GROUP)
-            def _(o):
-                t, p, device = member(o)
+        work(0, 2 * i)
+
+    send_fore(1)
+
+    @pl.when(z != 0)
+    def _():
+        edges[0].wait_recv()
+
+    @pl.when(z != DEPTH - 1)
+    def _():
+        edges[1].wait_recv()
+
+    @pl.loop(0, 2)
+    def _(step):
+        work(step, SLAB - 2)
+
+    send_fore(2)
+
+    def halo_copies(phase, times=pl.ds(0, ROWS)):
+        step, steps, place, places = PHASES[phase]
+        copies = []
+        for way, near, first, last, to in (
+            (0, above, SLAB - REACH - 1, SLAB - 1, SLAB),
+            (1, below, 0, REACH - 1, SLAB + REACH + 1),
+            (2, below, SLAB - 1, SLAB, SLAB + REACH),
+        ):
+            at, end = max(first, place), min(last, place + places)
+            if at < end:
+                copies.append(
+                    remote(
+                        mid.at[pl.ds(step, steps), times, pl.ds(at, end - at)],
+                        mid.at[pl.ds(step, steps), times, pl.ds(to + at - first, end - at)],
+                        halo_send.at[phase, way], halo_recv.at[phase, way], (tm, near),
+                    )
+                )
+        return copies
+
+    def wait_third(chip):
+        for p in range(PAIR):
+            source = 2 * chip - 1
+            own = jnp.logical_and(tm == source, pair == p)
+
+            @pl.when(own)
+            def _():
+                own_third().wait()
+
+            @pl.when(jnp.logical_not(own))
+            def _():
+                landing = landing_third(source, p)
                 remote(
-                    fore.at[t * PAIR + p, step], landing_fore(step, tm, pair),
-                    fore_send.at[step], fore_recv.at[step, o], device,
-                ).start()
-
-            own_fore(step).start()
-
-    def halo_copies(step, times=pl.ds(0, ROWS)):
-        return [
-            remote(
-                mid.at[step, times, pl.ds(at, count)], mid.at[step, times, pl.ds(to, count)],
-                halo_send.at[step, way], halo_recv.at[step, way], (tm, near),
-            )
-            for way, near, at, to, count in (
-                (0, above, SLAB - REACH - 1, SLAB, REACH),
-                (1, below, 0, SLAB + REACH + 1, REACH - 1),
-                (2, below, SLAB - 1, SLAB + REACH, 1),
-            )
-        ]
-
-    @pl.loop(0, 2 * GROUP // BATCH)
-    def _(i):
-        step, o0 = 1 - i // (GROUP // BATCH), lax.rem(i, GROUP // BATCH) * BATCH
-
-        @pl.when(o0 == 0)
-        def _():
-            own_fore(step).wait()
-
-        @pl.loop(0, BATCH)
-        def _(j):
-            @pl.when(o0 + j > 0)
-            def _():
-                t, p, device = member(o0 + j)
-                landing = landing_fore(step, t, p)
-                remote(
-                    landing, landing, fore_send.at[step], fore_recv.at[step, o0 + j], device
+                    landing, landing, third_send.at[0], third_recv.at[source // 2, p],
+                    (source, p * DEPTH + z),
                 ).wait_recv()
 
-        chip = member(o0)[0] // 2
-
-        @pl.when(jnp.logical_and(step == 0, chip > 0))
-        def _():
-            for p in range(PAIR):
-                source = 2 * chip - 1
-                own = jnp.logical_and(tm == source, pair == p)
-
-                @pl.when(own)
+    for phase, (step, steps, place, places) in enumerate(PHASES):
+        own_fore(phase).wait()
+        here = pl.ds(place, places)
+
+        @pl.loop(0, GROUP // BATCH)
+        def _(i):
+            @pl.loop(0, BATCH)
+            def _(j):
+                o = i * BATCH + j
+
+                @pl.when(o > 0)
                 def _():
-                    own_third().wait()
-
-                @pl.when(jnp.logical_not(own))
+                    t, p, device = member(o)
+                    landing = landing_fore(phase, t, p)
+                    remote(
+                        landing, landing, fore_send.at[phase], fore_recv.at[phase, o], device
+                    ).wait_recv()
+
+            chip = member(i * BATCH)[0] // 2
+            if step == 0:
+                @pl.when(chip > 0)
                 def _():
-                    landing = landing_third(source, p)
-                    remote(
-                        landing, landing, third_send.at[0], third_recv.at[source // 2, p],
-                        (source, p * DEPTH + z),
-                    ).wait_recv()
-
-            mid[0, 2 * chip, own_places] = mid[0, 2 * chip, own_places] + mid3[chip - 1]
-
-        for copy in halo_copies(step, pl.ds(2 * chip, 2)):
-            copy.start()
+                    if place == 0:
+                        wait_third(chip)
+                    mid[0, 2 * chip, here] = mid[0, 2 * chip, here] + mid3[chip - 1, here]
+
+            for copy in halo_copies(phase, pl.ds(2 * chip, 2)):
+                copy.start()
 
     @pl.when(extra)
     def _():
@@ -409,8 +442,8 @@
     def _(i):
         @pl.when(i == SLAB)
         def _():
-            for step in (1, 0):
-                for copy in halo_copies(step):
+            for phase in range(len(PHASES)):
+                for copy in halo_copies(phase):
                     copy.wait_recv()
 
         before, after = jnp.logical_and(i >= SLAB, i < SLAB + REACH), i >= SLAB + REACH
@@ -473,7 +506,7 @@
 
     def own_back(chunk):
         return pltpu.make_async_copy(
-            leaving(chunk, tm, pair), landing_back(chunk, tm, pair), own_sem.at[2 + chunk]
+            leaving(chunk, tm, pair), landing_back(chunk, tm, pair), own_sem.at[3 + chunk]
         )
 
     @pl.loop(0, CHUNKS)
@@ -556,11 +589,11 @@
         sent = third.at[others]
         remote(sent, sent, third_send.at[0], third_recv.at[0, 0], (tm, above)).wait_send()
 
-    for step in (1, 0):
-        for copy in halo_copies(step):
+    for phase, (step, steps, place, places) in enumerate(PHASES):
+        for copy in halo_copies(phase):
             copy.wait_send()
-        sent = fore.at[others, step]
-        remote(sent, sent, fore_send.at[step], fore_recv.at[step, 0], (tm, above)).wait_send()
+        sent = fore.at[others, pl.ds(step, steps), pl.ds(place, places)]
+        remote(sent, sent, fore_send.at[phase], fore_recv.at[phase, 0], (tm, above)).wait_send()
     for chunk in range(CHUNKS):
         sent = ret.at[others, :, planes_of(chunk)]
         remote(sent, sent, back_send.at[chunk], back_recv.at[chunk, 0], (tm, above)).wait_send()
@@ -597,18 +630,18 @@
             pltpu.VMEM(ymat.shape, jnp.bfloat16),
             pltpu.SMEM(table.shape, f32),
             pltpu.SemaphoreType.DMA((6,)),
-            pltpu.SemaphoreType.DMA((3 + CHUNKS,)),
+            pltpu.SemaphoreType.DMA((4 + CHUNKS,)),
             pltpu.SemaphoreType.DMA((1 + CHUNKS,)),
             pltpu.SemaphoreType.DMA((2,)),
             pltpu.SemaphoreType.DMA((2,)),
             pltpu.SemaphoreType.DMA((1,)),
             pltpu.SemaphoreType.DMA((1,)),
-            pltpu.SemaphoreType.DMA((steps,)),
-            pltpu.SemaphoreType.DMA((steps, GROUP)),
+            pltpu.SemaphoreType.DMA((len(PHASES),)),
+            pltpu.SemaphoreType.DMA((len(PHASES), GROUP)),
             pltpu.SemaphoreType.DMA((1,)),
             pltpu.SemaphoreType.DMA((ROWS // 2, PAIR)),
-            pltpu.SemaphoreType.DMA((steps, 3)),
-            pltpu.SemaphoreType.DMA((steps, 3)),
+            pltpu.SemaphoreType.DMA((len(PHASES), 3)),
+            pltpu.SemaphoreType.DMA((len(PHASES), 3)),
             pltpu.SemaphoreType.DMA((CHUNKS,)),
             pltpu.SemaphoreType.DMA((CHUNKS, GROUP)),
         ],

time: 65.5 us -> 63.2 us (0.965)
  Pallas kernels: 61.4 us -> 58.8 us
    pallas_call x1, Pallas kernels: 61.4 us -> 58.8 us  [body(): pl.pallas_call(kernel, out_shape=(whole, whole), in_specs=[hbm] * 7, out_...]
where the time goes in v4:
time: 63.2 us; the launch traced here: 62.8 us
  Pallas kernels  58.8 us (93%)
  local copies, waits for them, and re-layouts  3.36 us (5%)
  between operations  0.65 us (1%)
    pallas_call x1, Pallas kernels, body(): pl.pallas_call(kernel, out_shape=(whole, whole), in_specs=[hbm] * 7, out_...  58.8 us
    unnamed x4, local copies, waits for them, and re-layouts  3.36 us

profile of v4, /device:TPU:1, one launch (start us, length us, event | category | flops | bytes accessed | tf_op | source)
XLA Modules:
  0.0 62.8 jit_solution(3588609320923982190)
XLA Ops:
  0.6 58.8 %shard_map.86 = (f32[2,8,64,256]{3,2,1,0:T(8,128)}, f32[2,8,64,256]{3,2,1,0:T(8,128)}) custom-call(f32[2,8,64,256]{3,2,1,0:T(8,128)} %state.1, f32[8,64,256]{2,1,0:T(8,128)} %initial.1, f32[32,8,128]{2,1,0:T(8,128)} %constant.10.clone.mu_all, bf16[2,256,256]{2,1,0:T(8,128)(2,1)} %constant.11.clone.zf_all, bf16[2,256,256]{2,1,0:T(8,128)(2,1)} %constant.12.clone.zb_all, ...), custom_call_target="tpu_custom_call" | custom-call | flops 1000000000 | bytes 8388608 | tf_op jit(solution)/shard_map/pallas_call | solution.py:610
  59.4 0.0 copy-start
  59.4 2.4 %copy.11 = f32[2,8,64,256]{3,2,1,0:T(8,128)} copy(f32[2,8,64,256]{3,2,1,0:T(8,128)} %get-tuple-element.4) | data formatting | bytes 2097152
  61.8 0.0 copy-done
  61.8 1.0 %copy.12 = f32[2,8,64,256]{3,2,1,0:T(8,128)} copy(f32[2,8,64,256]{3,2,1,0:T(8,128)S(1)} %copy-done) | data formatting | bytes 2097152
Async XLA Ops:
  59.4 2.4 %copy-start = (f32[2,8,64,256]{3,2,1,0:T(8,128)S(1)}, f32[2,8,64,256]{3,2,1,0:T(8,128)}, u32[]{:S(2)}) copy-start(f32[2,8,64,256]{3,2,1,0:T(8,128)} %get-tuple-element.5) | copy-start | bytes 3145732

commit v5 on v4

--- a/solution.py
+++ b/solution.py
@@ -23,7 +23,7 @@
 HALF = SUB // PAIR
 REAL = (STEPS // 2 - 1) * 2 * SWEEPS
 GAMMA = REAL + 2 * SWEEPS
-CHUNKS = 2
+CHUNKS = 4
 OWN = SLAB // 2
 PHASES = ((1, 1, 0, SLAB - 2), (0, 1, 0, SLAB - 2), (0, 2, SLAB - 2, 2))
 BATCH = 2 * PAIR
@@ -241,7 +241,8 @@
             + pltpu.roll(s, 1, 1) + pltpu.roll(s, NZ - 1, 1)
         )
         laplace = couple_first * (near - 2.0 * s) + couple_cross * (cross - 4.0 * s)
-        return st[step, x + 1] - s + laplace + time_step * (s - s * s * s)
+        rest = st[step, x + 1] + laplace + time_step * (s - s * s * s)
+        return rest - s, rest
 
     def along_y(which, value):
         high, low = split(value)
@@ -296,8 +297,8 @@
         rows = []
         for j in range(2):
             x = lax.rem(place + j + 1, SLAB)
-            value = residual_of(step, x)
-            res[step, x] = value
+            value, rest = residual_of(step, x)
+            res[step, x] = rest
             rows.append(along_y(0, value))
         rows = along_z(zf, jnp.concatenate(rows, axis=0)) * table[GAMMA + 2 * tm + step]
 
@@ -571,7 +572,7 @@
             scale = table[GAMMA + STEPS + 2 * tm + step]
             for j in range(2):
                 delta = along_y(1, value[j * NY : (j + 1) * NY])
-                upd[step, x0 + j] = st[step + 1, x0 + j + 1] + scale * delta
+                upd[step, x0 + j] = scale * delta
 
         out_upd(chunk).start()
 
@@ -607,7 +608,7 @@
     steps = STEPS // ROWS
     hbm = pl.BlockSpec(memory_space=pltpu.HBM)
     f32 = jnp.float32
-    return pl.pallas_call(
+    delta, rest = pl.pallas_call(
         kernel,
         out_shape=(whole, whole),
         in_specs=[hbm] * 7,
@@ -650,6 +651,7 @@
         ),
         cost_estimate=pl.CostEstimate(flops=10**9, bytes_accessed=8 * 2**20, transcendentals=0),
     )(state, initial, mu, zf, zb, ymat, table)
+    return state + delta, rest - state
 
 
 def solution(mesh):

time: 63.2 us -> 62.6 us (level)
  local copies, waits for them, and re-layouts: 3.36 us -> 0.01 us
  other arithmetic: 0 us -> 3.16 us
    unnamed x4 -> x2, local copies, waits for them, and re-layouts: 3.36 us -> 0.01 us
    sub x0 -> x1, other arithmetic: none -> 3.16 us  [body(): return (state + delta, rest - state)]
where the time goes in v5:
time: 62.6 us; the launch traced here: 62.4 us
  Pallas kernels  58.6 us (94%)
  other arithmetic  3.16 us (5%)
  between operations  0.65 us (1%)
    pallas_call x1, Pallas kernels, body(): pl.pallas_call(kernel, out_shape=(whole, whole), in_specs=[hbm] * 7, out_...  58.6 us
    sub x1, other arithmetic, body(): return (state + delta, rest - state)  3.16 us

profile of v5, /device:TPU:1, one launch (start us, length us, event | category | flops | bytes accessed | tf_op | source)
XLA Modules:
  0.0 62.4 jit_solution(10566401477316156855)
XLA Ops:
  0.6 0.0 copy-start
  0.6 58.6 %shard_map.86 = (f32[2,8,64,256]{3,2,1,0:T(8,128)}, f32[2,8,64,256]{3,2,1,0:T(8,128)}) custom-call(f32[2,8,64,256]{3,2,1,0:T(8,128)} %state.1, f32[8,64,256]{2,1,0:T(8,128)} %initial.1, f32[32,8,128]{2,1,0:T(8,128)} %constant.10.clone.mu_all, bf16[2,256,256]{2,1,0:T(8,128)(2,1)} %constant.11.clone.zf_all, bf16[2,256,256]{2,1,0:T(8,128)(2,1)} %constant.12.clone.zb_all, ...), custom_call_target="tpu_custom_call" | custom-call | flops 1000000000 | bytes 8388608 | tf_op jit(solution)/shard_map/pallas_call | solution.py:611
  59.3 0.0 copy-done
  59.3 3.2 %fusion = (f32[2,8,64,256]{3,2,1,0:T(8,128)}, f32[2,8,64,256]{3,2,1,0:T(8,128)}) fusion(f32[2,8,64,256]{3,2,1,0:T(8,128)} %get-tuple-element.5, f32[2,8,64,256]{3,2,1,0:T(8,128)S(1)} %copy-done, f32[2,8,64,256]{3,2,1,0:T(8,128)} %get-tuple-element.4), kind=kLoop, calls=%fused_computation | loop fusion | flops 524288 | bytes 5242880 | tf_op jit(solution)/shard_map/sub | solution.py:654
Async XLA Ops:
  0.6 58.6 %copy-start = (f32[2,8,64,256]{3,2,1,0:T(8,128)S(1)}, f32[2,8,64,256]{3,2,1,0:T(8,128)}, u32[]{:S(2)}) copy-start(f32[2,8,64,256]{3,2,1,0:T(8,128)} %state.1) | copy-start | bytes 3145732
